TPU v7x, 32 devices: a whole 2x2x4 slice. The times are simulated.
32 devices in a mesh: groups: 2 (over y), blk: 4 (over z), team: 2 (over x), head: 2 (over core).
Axes of the slice: x: 2, y: 2, z: 4, core: 2. Of those that a mesh axis runs over, the one named last changes fastest.
Arguments:
- queries: bfloat16 [768, 2560], P(('groups', 'blk', 'team'), 'head'), parts along dimension 0, may hold values from -8 to 8
- key_rows: bfloat16 [768, 2560], P(('groups', 'blk', 'team'), 'head'), parts along dimension 0, may hold values from -8 to 8
- value_rows: bfloat16 [768, 2560], P(('groups', 'blk', 'team'), 'head'), parts along dimension 0, may hold values from -6 to 6
Outputs:
- attended: bfloat16 [768, 2560], P(('groups', 'blk', 'team'), 'head'), parts along dimension 0
There are 2 independent parts, one for each index of `groups`. A program takes and returns all parts, laid end to end along the dimension named above; each array names one. Nothing has to cross between parts.
All inputs are finite; a program needn't handle non-finite values.
Results may differ from a plain program's by a relative error of at most 0.009.
Values may be sent and summed in bfloat16 or wider, within the bound.
A program may use at most 64 MiB of HBM per device.

v0:
```python
from functools import partial
import math

import jax
import jax.numpy as jnp
from jax import lax
from jax.sharding import PartitionSpec as P

HD = 128
T_DEV = 48


def attend_block(running, key_block, value_block, query_rows, score_scale):
    row_top, row_total, weighted = running
    scores = (
        jnp.einsum("qhd,khd->qhk", query_rows, key_block, preferred_element_type=jnp.float32)
        * score_scale
    )
    new_top = jnp.maximum(row_top, jnp.max(scores, axis=2))
    shrink = jnp.exp(row_top - new_top)
    weights = jnp.exp(scores - new_top[:, :, None])
    row_total = row_total * shrink + jnp.sum(weights, axis=2)
    weighted = weighted * shrink[:, :, None] + jnp.einsum(
        "qhk,khd->qhd",
        weights.astype(jnp.bfloat16),
        value_block,
        preferred_element_type=jnp.float32,
    )
    return (new_top, row_total, weighted)


def fold_piece(running, shard_piece, first_row, query_rows, score_scale):
    key_piece, value_piece = shard_piece
    piece_rows = key_piece.shape[0]
    block_rows = T_DEV
    local_heads = query_rows.shape[1]
    key_blocks = key_piece.reshape(piece_rows // block_rows, block_rows, local_heads, HD)
    value_blocks = value_piece.reshape(piece_rows // block_rows, block_rows, local_heads, HD)

    def one_block(current, block_pair):
        return (attend_block(current, block_pair[0], block_pair[1], query_rows, score_scale), None)

    running, unused = lax.scan(one_block, running, (key_blocks, value_blocks))
    return running


def local(queries, key_rows, value_rows):
    own_rows = queries.shape[0]
    local_heads = queries.shape[1] // HD
    score_scale = 1.0 / math.sqrt(HD)
    team_queries = lax.all_gather(queries, "team", axis=0, tiled=True)
    team_count = team_queries.shape[0]
    query_heads = team_queries.reshape(team_count, local_heads, HD)
    folder = partial(fold_piece, query_rows=query_heads, score_scale=score_scale)
    row_top, row_total, weighted = folder(
        (
            jnp.full((team_count, local_heads), -1e30, jnp.float32),
            jnp.zeros((team_count, local_heads), jnp.float32),
            jnp.zeros((team_count, local_heads, HD), jnp.float32),
        ),
        (
            lax.all_gather(key_rows, "blk", axis=0, tiled=True),
            lax.all_gather(value_rows, "blk", axis=0, tiled=True),
        ),
        jnp.int32(0),
    )
    swapped, member_tops, totals = (
        lax.all_to_all(
            weighted.reshape(team_count, local_heads * HD),
            "team",
            split_axis=0,
            concat_axis=0,
            tiled=True,
        ),
        lax.all_to_all(row_top, "team", split_axis=0, concat_axis=0, tiled=True),
        lax.all_to_all(row_total, "team", split_axis=0, concat_axis=0, tiled=True),
    )
    members = lax.axis_size("team")
    member_tops = member_tops.reshape(members, own_rows, local_heads)
    common_top = jnp.max(member_tops, axis=0)
    factor = jnp.exp(member_tops - common_top[None])
    row_sum = jnp.sum(factor * totals.reshape(members, own_rows, local_heads), axis=0)
    summed = jnp.sum(
        factor[:, :, :, None] * swapped.reshape(members, own_rows, local_heads, HD), axis=0
    )
    mixed_rows = summed / row_sum[:, :, None]
    return mixed_rows.reshape(own_rows, local_heads * HD).astype(jnp.bfloat16)


def solution(mesh):
    in_specs = (
        P(("groups", "blk", "team"), "head"),
        P(("groups", "blk", "team"), "head"),
        P(("groups", "blk", "team"), "head"),
    )
    out_specs = P(("groups", "blk", "team"), "head")
    return jax.shard_map(local, mesh=mesh, in_specs=in_specs, out_specs=out_specs, check_vma=False)
```

profile of v0, /device:TPU:0, one launch (start us, length us, event | category | flops | bytes accessed | tf_op | source)
XLA Modules:
  0.0 70.1 jit_solution(14824911914724854757)
XLA Ops:
  0.0 17.2 %all_gather.9 = bf16[192,1280]{1,0:T(8,128)(2,1)S(1)} all-gather(bf16[48,1280]{1,0:T(8,128)(2,1)} %param.6), channel_id=1, replica_groups=mesh['groups'=2,'blk'=4,'team'=2,'head'=2] {'blk'}, dimensions={0}, use_global_device_ids=true | all-gather | bytes 614400 | tf_op jit(solution)/shard_map/all_gather | solution.py:62
  17.6 0.8 %copy-done = bf16[48,1280]{1,0:T(8,128)(2,1)S(1)} copy-done((bf16[48,1280]{1,0:T(8,128)(2,1)S(1)}, bf16[48,1280]{1,0:T(8,128)(2,1)}, u32[]{:S(2)}) %copy-start) | copy-done | bytes 122904
  18.4 15.9 %all_gather.11 = bf16[192,1280]{1,0:T(8,128)(2,1)S(1)} all-gather(bf16[48,1280]{1,0:T(8,128)(2,1)S(1)} %copy-done), channel_id=1, replica_groups=mesh['groups'=2,'blk'=4,'team'=2,'head'=2] {'blk'}, dimensions={0}, use_global_device_ids=true | all-gather | bytes 614400 | tf_op jit(solution)/shard_map/all_gather | solution.py:63
  34.7 0.8 %copy-done.1 = bf16[48,1280]{1,0:T(8,128)(2,1)S(1)} copy-done((bf16[48,1280]{1,0:T(8,128)(2,1)S(1)}, bf16[48,1280]{1,0:T(8,128)(2,1)}, u32[]{:S(2)}) %copy-start.1) | copy-done | bytes 122904
  35.4 5.5 %all_gather.10 = bf16[96,1280]{1,0:T(8,128)(2,1)S(1)} all-gather(bf16[48,1280]{1,0:T(8,128)(2,1)S(1)} %copy-done.1), channel_id=1, replica_groups=mesh['groups'=2,'blk'=4,'team'=2,'head'=2] {'team'}, dimensions={0}, use_global_device_ids=true | all-gather | bytes 368640 | tf_op jit(solution)/shard_map/all_gather | solution.py:51
  41.4 3.1 %while.15 = (s32[]{:T(128)}, f32[96,10]{0,1:T(8,128)S(1)}, f32[96,10]{0,1:T(8,128)S(1)}, f32[96,10,128]{2,0,1:T(8,128)S(1)}, bf16[4,48,10,128]{3,1,2,0:T(8,128)(...) while((s32[]{:T(128)}, f32[96,10]{0,1:T(8,128)S(1)}, ...), condition=%wide.region_3.4_spmd.clone, body=%wide.region_0.3_spmd.clone.sunk | while | flops 24242884 | bytes 2159217 | solution.py:43
  41.8 0.3 fusion.29
  42.6 0.3 fusion.29
  43.4 0.3 fusion.29
  44.1 0.3 fusion.29
  44.6 0.7 reshape.41
  45.3 3.2 %all-to-all-start = ((f32[2,1,480]{2,1,0:T(1,128)}), f32[2,1,480]{2,1,0:T(1,128)S(1)}, u32[]{:S(2)}, u32[]{:S(2)}) async-start(f32[2,1,480]{2,1,0:T(1,128)} %reshape.41), calls=%async_computation | async-start | bytes 8192 | tf_op jit(solution)/shard_map/all_to_all | solution.py:75
  48.6 0.7 reshape.43
  49.3 3.0 %all-to-all-done = f32[2,1,480]{2,1,0:T(1,128)S(1)} async-done(((f32[2,1,480]{2,1,0:T(1,128)}), f32[2,1,480]{2,1,0:T(1,128)S(1)}, u32[]{:S(2)}, u32[]{:S(2)}) %all-to-all-start) | async-done | bytes 3872 | tf_op jit(solution)/shard_map/all_to_all | solution.py:75
  52.3 3.2 %all-to-all-start.2 = ((f32[2,1,480]{2,1,0:T(1,128)}), f32[2,1,480]{2,1,0:T(1,128)S(1)}, u32[]{:S(2)}, u32[]{:S(2)}) async-start(f32[2,1,480]{2,1,0:T(1,128)} %reshape.43), calls=%async_computation.2 | async-start | bytes 8192 | tf_op jit(solution)/shard_map/all_to_all | solution.py:76
  55.5 0.3 copy.25
  55.8 0.9 %all_to_all.20 = f32[2,48,1280]{2,1,0:T(8,128)} reshape(f32[96,10,128]{2,1,0:T(8,128)S(1)} %copy.25) | data formatting | bytes 983040 | tf_op jit(solution)/shard_map/all_to_all | solution.py:68
  56.7 0.5 broadcast.38
  57.2 0.7 reduce.2
  57.9 1.3 %all-to-all-done.2 = f32[2,1,480]{2,1,0:T(1,128)S(1)} async-done(((f32[2,1,480]{2,1,0:T(1,128)}), f32[2,1,480]{2,1,0:T(1,128)S(1)}, u32[]{:S(2)}, u32[]{:S(2)}) %all-to-all-start.2) | async-done | bytes 3872 | tf_op jit(solution)/shard_map/all_to_all | solution.py:76
  59.3 3.5 %all-to-all-start.1 = ((f32[2,48,1280]{2,1,0:T(8,128)}), f32[2,48,1280]{2,1,0:T(8,128)S(1)}, u32[]{:S(2)}, u32[]{:S(2)}) async-start(f32[2,48,1280]{2,1,0:T(8,128)} %all_to_all.20), calls=%async_computation.1 | async-start | bytes 983040 | tf_op jit(solution)/shard_map/all_to_all | solution.py:68
  62.8 0.7 reduce.3
  64.1 5.1 %all-to-all-done.1 = f32[2,48,1280]{2,1,0:T(8,128)S(1)} async-done(((f32[2,48,1280]{2,1,0:T(8,128)}), f32[2,48,1280]{2,1,0:T(8,128)S(1)}, u32[]{:S(2)}, u32[]{:S(2)}) %all-to-all-start.1) | async-done | bytes 491552 | tf_op jit(solution)/shard_map/all_to_all | solution.py:68
  69.4 0.7 %fusion.13 = bf16[48,1280]{1,0:T(8,128)(2,1)} fusion(f32[48,1280]{1,0:T(8,128)S(1)} %multiply_reduce_fusion, f32[6,8,10,128]{3,2,1,0:T(8,128)S(1)} %bitcast.44), kind=kLoop, calls=%fused_computation.21 | loop fusion | flops 122880 | bytes 614400 | tf_op jit(solution)/shard_map/convert_element_type | solution.py:87
  (45 shorter events, 3.8 us)
Async XLA Ops:
  17.5 0.9 %copy-start = (bf16[48,1280]{1,0:T(8,128)(2,1)S(1)}, bf16[48,1280]{1,0:T(8,128)(2,1)}, u32[]{:S(2)}) copy-start(bf16[48,1280]{1,0:T(8,128)(2,1)} %param.7) | copy-start | bytes 368644
  34.5 0.9 %copy-start.1 = (bf16[48,1280]{1,0:T(8,128)(2,1)S(1)}, bf16[48,1280]{1,0:T(8,128)(2,1)}, u32[]{:S(2)}) copy-start(bf16[48,1280]{1,0:T(8,128)(2,1)} %param.5) | copy-start | bytes 368644
  45.3 7.0 %all-to-all-start = ((f32[2,1,480]{2,1,0:T(1,128)}), f32[2,1,480]{2,1,0:T(1,128)S(1)}, u32[]{:S(2)}, u32[]{:S(2)}) async-start(f32[2,1,480]{2,1,0:T(1,128)} %reshape.41), calls=%async_computation | async-start | bytes 8192 | tf_op jit(solution)/shard_map/all_to_all | solution.py:75
  52.3 7.0 %all-to-all-start.2 = ((f32[2,1,480]{2,1,0:T(1,128)}), f32[2,1,480]{2,1,0:T(1,128)S(1)}, u32[]{:S(2)}, u32[]{:S(2)}) async-start(f32[2,1,480]{2,1,0:T(1,128)} %reshape.43), calls=%async_computation.2 | async-start | bytes 8192 | tf_op jit(solution)/shard_map/all_to_all | solution.py:76
  59.3 9.9 %all-to-all-start.1 = ((f32[2,48,1280]{2,1,0:T(8,128)}), f32[2,48,1280]{2,1,0:T(8,128)S(1)}, u32[]{:S(2)}, u32[]{:S(2)}) async-start(f32[2,48,1280]{2,1,0:T(8,128)} %all_to_all.20), calls=%async_computation.1 | async-start | bytes 983040 | tf_op jit(solution)/shard_map/all_to_all | solution.py:68
where the time goes:
time: 70.5 us; the launch traced here: 70.1 us
  blocking collectives  38.6 us (55%)
  starting transfers between devices  9.91 us (14%)
  waiting for transfers between devices  9.42 us (13%)
  local copies, waits for them, and re-layouts  6.86 us (10%)
  matrix products  2.52 us (4%)
  other arithmetic  2.46 us (3%)
    all_gather x1, blocking collectives, local(): lax.all_gather(key_rows, 'blk', axis=0, tiled=True)  17.2 us
    all_gather x1, blocking collectives, local(): lax.all_gather(value_rows, 'blk', axis=0, tiled=True)  15.9 us
    all_gather x1, blocking collectives, local(): team_queries = lax.all_gather(queries, 'team', axis=0, tiled=True)  5.54 us
    all_to_all x1, waiting for transfers between devices, local(): lax.all_to_all(weighted.reshape(team_count, local_heads * HD), 'team', sp...  5.06 us
    unnamed x11, local copies, waits for them, and re-layouts  3.5 us
    all_to_all x1, starting transfers between devices, local(): lax.all_to_all(weighted.reshape(team_count, local_heads * HD), 'team', sp...  3.48 us
    all_to_all x1, starting transfers between devices, local(): lax.all_to_all(row_top, 'team', split_axis=0, concat_axis=0, tiled=True)  3.22 us
    all_to_all x1, starting transfers between devices, local(): lax.all_to_all(row_total, 'team', split_axis=0, concat_axis=0, tiled=True)  3.21 us
  transfers between devices with their start and end apart: 3, of which 3 were waited for; matrix products, arithmetic and copies ran while one was open for 5% of the time, Pallas kernels for 0%

commit v1 on v0

v1 whole, which is shorter than its diff:
```python
from functools import partial
import math

import jax
import jax.numpy as jnp
from jax import lax
from jax.experimental import pallas as pl
from jax.experimental.pallas import tpu as pltpu
from jax.sharding import PartitionSpec as P

HD = 128
MESH = pl.DeviceIdType.MESH


def attend_block(running, key_block, value_block, query_rows, score_scale):
    row_top, row_total, weighted = running
    scores = (
        jnp.einsum("qhd,khd->qhk", query_rows, key_block, preferred_element_type=jnp.float32)
        * score_scale
    )
    new_top = jnp.maximum(row_top, jnp.max(scores, axis=2))
    shrink = jnp.exp(row_top - new_top)
    weights = jnp.exp(scores - new_top[:, :, None])
    row_total = row_total * shrink + jnp.sum(weights, axis=2)
    weighted = weighted * shrink[:, :, None] + jnp.einsum(
        "qhk,khd->qhd",
        weights.astype(jnp.bfloat16),
        value_block,
        preferred_element_type=jnp.float32,
    )
    return (new_top, row_total, weighted)


def gathered(queries, key_rows, value_rows):
    own_rows = queries.shape[0]
    local_heads = queries.shape[1] // HD
    score_scale = 1.0 / math.sqrt(HD)
    query_heads = queries.reshape(own_rows, local_heads, HD)
    axes = ("blk", "team")
    keys = lax.all_gather(key_rows, axes, axis=0, tiled=True)
    values = lax.all_gather(value_rows, axes, axis=0, tiled=True)
    blocks = keys.shape[0] // own_rows
    keys = keys.reshape(blocks, own_rows, local_heads, HD)
    values = values.reshape(blocks, own_rows, local_heads, HD)

    def one_block(current, block_pair):
        return (attend_block(current, *block_pair, query_heads, score_scale), None)

    (_, row_total, weighted), _ = lax.scan(
        one_block,
        (
            jnp.full((own_rows, local_heads), -1e30, jnp.float32),
            jnp.zeros((own_rows, local_heads), jnp.float32),
            jnp.zeros((own_rows, local_heads, HD), jnp.float32),
        ),
        (keys, values),
    )
    mixed = weighted / row_total[:, :, None]
    return mixed.reshape(own_rows, local_heads * HD).astype(jnp.bfloat16)


def attend(q, k, v):
    scores = lax.dot_general(
        q, k, (((1,), (1,)), ((), ())), preferred_element_type=jnp.float32
    ) * (1.0 / math.sqrt(HD))
    top = jnp.max(scores, axis=1, keepdims=True)
    weights = jnp.exp(scores - top)
    total = jnp.sum(weights, axis=1, keepdims=True)
    mixed = jnp.dot(weights.astype(jnp.bfloat16), v, preferred_element_type=jnp.float32)
    return (mixed / total).astype(jnp.bfloat16)


def exchange_kernel(
    members, teams, whole, rest,
    q_ref, k_ref, v_ref, out_ref,
    qw, kw, vw, ow, qr, kr, vr, orest,
    send_sem, out_send_sem, recv_sem, rest_sem, out_sem,
):
    rows = q_ref.shape[0]
    me = lax.axis_index("blk") * teams + lax.axis_index("team")
    share = members // rest if rest else 0

    def where(member):
        return {"blk": member // teams, "team": member % teams}

    def at_rows(block):
        return pl.ds(pl.multiple_of(block * rows, rows), rows)

    def head_cols(head):
        return pl.ds(pl.multiple_of(head * HD, HD), HD)

    steps = sorted(range(1, members), key=lambda s: -min(s, members - s))
    others = [lax.rem(me + s, members) for s in steps]

    barrier = pltpu.get_barrier_semaphore()
    for other in others:
        pl.semaphore_signal(barrier, inc=1, device_id=where(other), device_id_type=MESH)
    for g in range(whole):
        for a, (src, dst) in enumerate(((k_ref, kw), (q_ref, qw), (v_ref, vw))):
            pltpu.make_async_copy(
                src.at[:, head_cols(me * whole + g)], dst.at[g, at_rows(me), :], recv_sem.at[a]
            ).start()
    if rest:
        mine = me // share
        for a, (src, dst) in enumerate(((k_ref, kr), (v_ref, vr))):
            pltpu.make_async_copy(
                src.at[:, head_cols(members * whole + mine)], dst.at[at_rows(me), :], rest_sem.at[a]
            ).start()
    pl.semaphore_wait(barrier, members - 1)

    sent = []

    def send(src, dst, sem, member):
        copy = pltpu.make_async_remote_copy(
            src_ref=src, dst_ref=dst, send_sem=send_sem, recv_sem=sem,
            device_id=where(member), device_id_type=MESH,
        )
        copy.start()
        sent.append(copy)

    for a, (src, dst) in enumerate(((k_ref, kw), (q_ref, qw), (v_ref, vw))):
        for other in others:
            for g in range(whole):
                send(
                    src.at[:, head_cols(other * whole + g)], dst.at[g, at_rows(me), :],
                    recv_sem.at[a], other,
                )
    if rest:
        part, slot = me // rest, me % rest
        for r in range(rest):
            owner = r * share + part
            src = q_ref.at[:, head_cols(members * whole + r)]
            dst = qr.at[at_rows(slot), :]

            @pl.when(owner == me)
            def _():
                pltpu.make_async_copy(src, dst, rest_sem.at[2]).start()

            @pl.when(owner != me)
            def _():
                pltpu.make_async_remote_copy(
                    src_ref=src, dst_ref=dst, send_sem=send_sem, recv_sem=rest_sem.at[2],
                    device_id=where(owner), device_id_type=MESH,
                ).start()
        for a, (src, dst) in enumerate(((k_ref, kr), (v_ref, vr))):
            for other in others:
                send(
                    src.at[:, head_cols(members * whole + other // share)], dst.at[at_rows(me), :],
                    rest_sem.at[a], other,
                )

    def arrived(ref, sem):
        pltpu.make_async_copy(ref, ref, sem).wait()

    def give(src, block, head):
        dst = out_ref.at[:, head_cols(head)]

        @pl.when(block == me)
        def _():
            pltpu.make_async_copy(src, dst, out_sem).start()

        @pl.when(block != me)
        def _():
            pltpu.make_async_remote_copy(
                src_ref=src, dst_ref=dst, send_sem=out_send_sem, recv_sem=out_sem,
                device_id=where(block), device_id_type=MESH,
            ).start()

    for a, ref in enumerate((kw, qw, vw)):
        arrived(ref, recv_sem.at[a])
    chunk = 2 if members % 2 == 0 else 1
    for g in range(whole):
        for c in range(0, members, chunk):
            span = pl.ds(c * rows, chunk * rows)
            ow[g, span, :] = attend(qw[g, span, :], kw[g], vw[g])
            for b in range(c, c + chunk):
                give(ow.at[g, pl.ds(b * rows, rows), :], jnp.int32(b), me * whole + g)
    if rest:
        for a, ref in enumerate((kr, vr, qr)):
            arrived(ref, rest_sem.at[a])
        orest[...] = attend(qr[...], kr[...], vr[...])
        for b in range(rest):
            give(
                orest.at[pl.ds(b * rows, rows), :], (me % share) * rest + b,
                members * whole + me // share,
            )

    for copy in sent:
        copy.wait_send()
    if rest:
        for r in range(rest):
            @pl.when(r * share + me // rest != me)
            def _():
                block = qr.at[pl.ds(0, rows), :]
                pltpu.make_async_copy(block, block, send_sem).wait()
    for b in range(members):
        @pl.when(b != me)
        def _():
            block = ow.at[:, pl.ds(0, rows), :]
            pltpu.make_async_copy(block, block, out_send_sem).wait()
    for b in range(rest):
        @pl.when((me % share) * rest + b != me)
        def _():
            block = orest.at[pl.ds(0, rows), :]
            pltpu.make_async_copy(block, block, out_send_sem).wait()
    arrived(out_ref, out_sem)


def exchanged(queries, key_rows, value_rows, *, teams, members, whole, rest):
    rows, columns = queries.shape
    bf16 = jnp.bfloat16
    full = pltpu.VMEM((whole, members * rows, HD), bf16)
    rest_full = pltpu.VMEM((members * rows, HD), bf16)
    rest_part = pltpu.VMEM((max(rest, 1) * rows, HD), bf16)
    return pl.pallas_call(
        partial(exchange_kernel, members, teams, whole, rest),
        out_shape=jax.ShapeDtypeStruct((rows, columns), bf16),
        in_specs=[pl.BlockSpec(memory_space=pl.ANY)] * 3,
        out_specs=pl.BlockSpec(memory_space=pl.ANY),
        scratch_shapes=[
            full, full, full, full, rest_part, rest_full, rest_full, rest_part,
            pltpu.SemaphoreType.DMA,
            pltpu.SemaphoreType.DMA,
            pltpu.SemaphoreType.DMA((3,)),
            pltpu.SemaphoreType.DMA((3,)),
            pltpu.SemaphoreType.DMA,
        ],
        compiler_params=pltpu.CompilerParams(collective_id=0, has_side_effects=True),
    )(queries, key_rows, value_rows)


def solution(mesh):
    teams, members = mesh.shape["team"], mesh.shape["blk"] * mesh.shape["team"]

    def local(queries, key_rows, value_rows):
        heads = queries.shape[1] // HD
        whole, rest = heads // members, heads % members
        if whole >= 1 and (rest == 0 or members % rest == 0):
            return exchanged(
                queries, key_rows, value_rows,
                teams=teams, members=members, whole=whole, rest=rest,
            )
        return gathered(queries, key_rows, value_rows)

    spec = P(("groups", "blk", "team"), "head")
    return jax.shard_map(
        local, mesh=mesh, in_specs=(spec,) * 3, out_specs=spec, check_vma=False
    )
```

time: 70.5 us -> 24.3 us (0.34)
  blocking collectives: 38.6 us -> 0 us
  Pallas kernels: 0 us -> 22.6 us
  starting transfers between devices: 9.91 us -> 0 us
  waiting for transfers between devices: 9.42 us -> 0 us
  local copies, waits for them, and re-layouts: 6.86 us -> 1.56 us
  matrix products: 2.52 us -> 0 us
  other arithmetic: 2.46 us -> 0 us
    all_gather x3 -> x0, blocking collectives: 38.6 us -> none  [the longest x1 17.2 us: local(): lax.all_gather(key_rows, 'blk', axis=0, tiled=True)]
    pallas_call x0 -> x1, Pallas kernels: none -> 22.6 us  [exchanged(): pl.pallas_call(partial(exchange_kernel, members, teams, whole, rest), out...]
    all_to_all x3 -> x0, starting transfers between devices: 9.91 us -> none  [the longest x1 3.48 us: local(): lax.all_to_all(weighted.reshape(team_count, local_heads * HD), 'team', sp...]
    all_to_all x3 -> x0, waiting for transfers between devices: 9.42 us -> none  [the longest x1 5.06 us: local(): lax.all_to_all(weighted.reshape(team_count, local_heads * HD), 'team', sp...]
    dot_general x8 -> x0, matrix products: 2.52 us -> none  [the longest x4 1.37 us: attend_block(): jnp.einsum('qhk,khd->qhd', weights.astype(jnp.bfloat16), value_block, pre...]
    unnamed x11 -> x1, local copies, waits for them, and re-layouts: 3.5 us -> 1.56 us
    all_to_all x6 -> x0, local copies, waits for them, and re-layouts: 1.53 us -> none  [the longest x1 0.86 us: local(): lax.all_to_all(weighted.reshape(team_count, local_heads * HD), 'team', sp...]
    all_to_all x2 -> x0, other arithmetic: 1.33 us -> none  [the longest x1 0.67 us: local(): lax.all_to_all(row_total, 'team', split_axis=0, concat_axis=0, tiled=True)]
  transfers between devices with their start and end apart: 3 -> 0, of which waited for: 3 -> 0; matrix products, arithmetic and copies ran while one was open for 5% -> 0% of each run, Pallas kernels for 0% -> 0%
where the time goes in v1:
time: 24.3 us; the launch traced here: 24.2 us
  Pallas kernels  22.6 us (93%)
  local copies, waits for them, and re-layouts  1.56 us (6%)
    pallas_call x1, Pallas kernels, exchanged(): pl.pallas_call(partial(exchange_kernel, members, teams, whole, rest), out...  22.6 us
    unnamed x1, local copies, waits for them, and re-layouts  1.56 us

profile of v1, /device:TPU:0, one launch (start us, length us, event | category | flops | bytes accessed | tf_op | source)
XLA Modules:
  0.0 24.2 jit_solution(9628582160655339369)
XLA Ops:
  0.0 22.6 %shard_map.37 = bf16[48,1280]{1,0:T(8,128)(2,1)} custom-call(bf16[48,1280]{1,0:T(8,128)(2,1)} %q_ref.1, bf16[48,1280]{1,0:T(8,128)(2,1)} %k_ref.1, bf16[48,1280]{1,0:T(8,128)(2,1)} %v_ref.1), custom_call_target="tpu_custom_call" | custom-call | tf_op jit(solution)/shard_map/pallas_call | solution.py:215
  22.6 1.6 %copy.5 = bf16[48,1280]{1,0:T(8,128)(2,1)} copy(bf16[48,1280]{1,0:T(8,128)(2,1)} %shard_map.37) | data formatting | bytes 245760

commit v2 on v1

v2 whole, which is shorter than its diff:
```python
from functools import partial
import math

import jax
import jax.numpy as jnp
from jax import lax
from jax.experimental import pallas as pl
from jax.experimental.pallas import tpu as pltpu
from jax.sharding import PartitionSpec as P

HD = 128
MESH = pl.DeviceIdType.MESH


def attend_block(running, key_block, value_block, query_rows, score_scale):
    row_top, row_total, weighted = running
    scores = (
        jnp.einsum("qhd,khd->qhk", query_rows, key_block, preferred_element_type=jnp.float32)
        * score_scale
    )
    new_top = jnp.maximum(row_top, jnp.max(scores, axis=2))
    shrink = jnp.exp(row_top - new_top)
    weights = jnp.exp(scores - new_top[:, :, None])
    row_total = row_total * shrink + jnp.sum(weights, axis=2)
    weighted = weighted * shrink[:, :, None] + jnp.einsum(
        "qhk,khd->qhd",
        weights.astype(jnp.bfloat16),
        value_block,
        preferred_element_type=jnp.float32,
    )
    return (new_top, row_total, weighted)


def gathered(queries, key_rows, value_rows):
    own_rows = queries.shape[0]
    local_heads = queries.shape[1] // HD
    score_scale = 1.0 / math.sqrt(HD)
    query_heads = queries.reshape(own_rows, local_heads, HD)
    axes = ("blk", "team")
    keys = lax.all_gather(key_rows, axes, axis=0, tiled=True)
    values = lax.all_gather(value_rows, axes, axis=0, tiled=True)
    blocks = keys.shape[0] // own_rows
    keys = keys.reshape(blocks, own_rows, local_heads, HD)
    values = values.reshape(blocks, own_rows, local_heads, HD)

    def one_block(current, block_pair):
        return (attend_block(current, *block_pair, query_heads, score_scale), None)

    (_, row_total, weighted), _ = lax.scan(
        one_block,
        (
            jnp.full((own_rows, local_heads), -1e30, jnp.float32),
            jnp.zeros((own_rows, local_heads), jnp.float32),
            jnp.zeros((own_rows, local_heads, HD), jnp.float32),
        ),
        (keys, values),
    )
    mixed = weighted / row_total[:, :, None]
    return mixed.reshape(own_rows, local_heads * HD).astype(jnp.bfloat16)


def attend(q, k, v):
    scores = lax.dot_general(
        q, k, (((1,), (1,)), ((), ())), preferred_element_type=jnp.float32
    ) * (1.0 / math.sqrt(HD))
    top = jnp.max(scores, axis=1, keepdims=True)
    weights = jnp.exp(scores - top)
    total = jnp.sum(weights, axis=1, keepdims=True)
    mixed = jnp.dot(weights.astype(jnp.bfloat16), v, preferred_element_type=jnp.float32)
    return (mixed / total).astype(jnp.bfloat16)


def exchange_kernel(
    blks, teams, cores, whole, rest,
    q_ref, k_ref, v_ref, out_ref,
    qw, kw, vw, ow, qr, kvr, orest,
    send_sem, out_send_sem, recv_sem, direct_sem, passed_sem, rest_q_sem, out_sem,
):
    rows = q_ref.shape[0]
    members = blks * teams
    blk, team, core = lax.axis_index("blk"), lax.axis_index("team"), lax.axis_index("head")
    me = blk * teams + team

    def where(member, on_core=core):
        return {"blk": member // teams, "team": member % teams, "head": on_core}

    def at_rows(block):
        return pl.ds(pl.multiple_of(block * rows, rows), rows)

    def head_cols(head):
        return pl.ds(pl.multiple_of(head * HD, HD), HD)

    steps = sorted(range(1, members), key=lambda s: -min(s, members - s))
    others = [lax.rem(me + s, members) for s in steps]

    barrier = pltpu.get_barrier_semaphore()
    greeted = cores if rest else 1
    for turn in range(greeted):
        on_core = lax.rem(core + turn, cores)
        for other in others + ([me] if turn else []):
            pl.semaphore_signal(
                barrier, inc=1, device_id=where(other, on_core), device_id_type=MESH
            )
    for g in range(whole):
        for a, (src, dst) in enumerate(((k_ref, kw), (q_ref, qw), (v_ref, vw))):
            pltpu.make_async_copy(
                src.at[:, head_cols(me * whole + g)], dst.at[g, at_rows(me), :], recv_sem.at[a]
            ).start()
    pl.semaphore_wait(barrier, members * greeted - 1)

    def put(src, dst, here, device, sends, sem):
        @pl.when(here)
        def _():
            pltpu.make_async_copy(src, dst, sem).start()

        @pl.when(jnp.logical_not(here))
        def _():
            pltpu.make_async_remote_copy(
                src_ref=src, dst_ref=dst, send_sem=sends, recv_sem=sem,
                device_id=device, device_id_type=MESH,
            ).start()

    def arrived(ref, sem):
        pltpu.make_async_copy(ref, ref, sem).wait()

    part, slot = (me // rest, me % rest) if rest else (0, 0)
    for r in range(rest):
        home = core * rest + r
        cols = head_cols(members * whole + r)
        for a, src in enumerate((k_ref, v_ref)):
            put(
                src.at[:, cols], kvr.at[a, at_rows(me), :], home == blk,
                where(home * teams + team), send_sem, direct_sem.at[blk],
            )
        put(
            q_ref.at[:, cols], qr.at[at_rows(slot), :],
            (home == blk) & (part == team * cores + core),
            where(home * teams + part // cores, part % cores), send_sem, rest_q_sem,
        )
    sent = []
    for a, (src, dst) in enumerate(((k_ref, kw), (q_ref, qw), (v_ref, vw))):
        for other in others:
            for g in range(whole):
                copy = pltpu.make_async_remote_copy(
                    src_ref=src.at[:, head_cols(other * whole + g)],
                    dst_ref=dst.at[g, at_rows(me), :],
                    send_sem=send_sem, recv_sem=recv_sem.at[a],
                    device_id=where(other), device_id_type=MESH,
                )
                copy.start()
                sent.append(copy)

    if rest:
        @pl.when(blk // rest == core)
        def _():
            for b in range(blks):
                block = kvr.at[:, at_rows(b * teams + team), :]
                arrived(block, direct_sem.at[b])
                for turn in range(1, teams * cores):
                    t = lax.rem(team + turn // cores, teams)
                    pltpu.make_async_remote_copy(
                        src_ref=block, dst_ref=block, send_sem=send_sem, recv_sem=passed_sem,
                        device_id=where(blk * teams + t, lax.rem(core + turn % cores, cores)),
                        device_id_type=MESH,
                    ).start()

    for a, ref in enumerate((kw, qw, vw)):
        arrived(ref, recv_sem.at[a])
    chunk = 2 if members % 2 == 0 else 1
    for g in range(whole):
        for c in range(0, members, chunk):
            span = pl.ds(c * rows, chunk * rows)
            ow[g, span, :] = attend(qw[g, span, :], kw[g], vw[g])
            for b in range(c, c + chunk):
                put(
                    ow.at[g, pl.ds(b * rows, rows), :], out_ref.at[:, head_cols(me * whole + g)],
                    b == me, where(b), out_send_sem, out_sem,
                )
    first = (team * cores + core) * rest
    if rest:
        @pl.when(blk // rest == core)
        def _():
            if teams > 1:
                arrived(kvr.at[:, pl.ds(0, (teams - 1) * blks * rows), :], passed_sem)

        @pl.when(blk // rest != core)
        def _():
            arrived(kvr, passed_sem)

        arrived(qr, rest_q_sem)
        orest[...] = attend(qr[...], kvr[0], kvr[1])
        for b in range(rest):
            put(
                orest.at[pl.ds(b * rows, rows), :],
                out_ref.at[:, head_cols(members * whole + blk % rest)],
                (blk // rest == core) & (first + b == me),
                where(first + b, blk // rest), out_send_sem, out_sem,
            )

    for copy in sent:
        copy.wait_send()
    tile = ow.at[0, pl.ds(0, rows), :]
    for r in range(rest):
        home = core * rest + r

        @pl.when(home != blk)
        def _():
            for _ in range(2):
                arrived(tile, send_sem)

        @pl.when((home != blk) | (part != team * cores + core))
        def _():
            arrived(tile, send_sem)
    if rest:
        @pl.when(blk // rest == core)
        def _():
            for _ in range(teams * cores - 1):
                arrived(kvr.at[:, pl.ds(0, blks * rows), :], send_sem)
    for b in range(members):
        @pl.when(b != me)
        def _():
            arrived(ow.at[:, pl.ds(0, rows), :], out_send_sem)
    for b in range(rest):
        @pl.when((blk // rest != core) | (first + b != me))
        def _():
            arrived(tile, out_send_sem)
    arrived(out_ref, out_sem)


def exchanged(queries, key_rows, value_rows, *, blks, teams, cores, whole, rest):
    rows, columns = queries.shape
    members = blks * teams
    bf16 = jnp.bfloat16
    full = pltpu.VMEM((whole, members * rows, HD), bf16)
    rest_part = pltpu.VMEM((max(rest, 1) * rows, HD), bf16)
    return pl.pallas_call(
        partial(exchange_kernel, blks, teams, cores, whole, rest),
        out_shape=jax.ShapeDtypeStruct((rows, columns), bf16),
        in_specs=[pl.BlockSpec(memory_space=pl.ANY)] * 3,
        out_specs=pl.BlockSpec(memory_space=pl.ANY),
        scratch_shapes=[
            full, full, full, full,
            rest_part, pltpu.VMEM((2, members * rows, HD), bf16), rest_part,
            pltpu.SemaphoreType.DMA,
            pltpu.SemaphoreType.DMA,
            pltpu.SemaphoreType.DMA((3,)),
            pltpu.SemaphoreType.DMA((blks,)),
            pltpu.SemaphoreType.DMA,
            pltpu.SemaphoreType.DMA,
            pltpu.SemaphoreType.DMA,
        ],
        compiler_params=pltpu.CompilerParams(collective_id=0, has_side_effects=True),
    )(queries, key_rows, value_rows)


def solution(mesh):
    blks, teams, cores = (mesh.shape[name] for name in ("blk", "team", "head"))

    def local(queries, key_rows, value_rows):
        heads = queries.shape[1] // HD
        whole, rest = heads // (blks * teams), heads % (blks * teams)
        if whole >= 1 and rest * cores in (0, blks):
            return exchanged(
                queries, key_rows, value_rows,
                blks=blks, teams=teams, cores=cores, whole=whole, rest=rest,
            )
        return gathered(queries, key_rows, value_rows)

    spec = P(("groups", "blk", "team"), "head")
    return jax.shard_map(
        local, mesh=mesh, in_specs=(spec,) * 3, out_specs=spec, check_vma=False
    )
```

time: 24.3 us -> 22.7 us (0.934); the launches traced: 24.2 us -> 22.3 us
  Pallas kernels: 22.6 us -> 20.7 us
    pallas_call x1, Pallas kernels: 22.6 us -> 20.7 us  [exchanged(): pl.pallas_call(partial(exchange_kernel, blks, teams, cores, whole, rest),...]
where the time goes in v2:
time: 22.7 us; the launch traced here: 22.3 us
  Pallas kernels  20.7 us (91%)
  local copies, waits for them, and re-layouts  1.56 us (7%)
    pallas_call x1, Pallas kernels, exchanged(): pl.pallas_call(partial(exchange_kernel, blks, teams, cores, whole, rest),...  20.7 us
    unnamed x1, local copies, waits for them, and re-layouts  1.56 us

profile of v2, /device:TPU:0, one launch (start us, length us, event | category | flops | bytes accessed | tf_op | source)
XLA Modules:
  0.0 22.3 jit_solution(13600396966568372892)
XLA Ops:
  0.0 20.7 %shard_map.37 = bf16[48,1280]{1,0:T(8,128)(2,1)} custom-call(bf16[48,1280]{1,0:T(8,128)(2,1)} %q_ref.1, bf16[48,1280]{1,0:T(8,128)(2,1)} %k_ref.1, bf16[48,1280]{1,0:T(8,128)(2,1)} %v_ref.1), custom_call_target="tpu_custom_call" | custom-call | tf_op jit(solution)/shard_map/pallas_call | solution.py:236
  20.7 1.6 %copy.5 = bf16[48,1280]{1,0:T(8,128)(2,1)} copy(bf16[48,1280]{1,0:T(8,128)(2,1)} %shard_map.37) | data formatting | bytes 245760

commit v3 on v2

--- a/solution.py
+++ b/solution.py
@@ -59,21 +59,24 @@
     return mixed.reshape(own_rows, local_heads * HD).astype(jnp.bfloat16)
 
 
-def attend(q, k, v):
+def soften(q, k):
     scores = lax.dot_general(
         q, k, (((1,), (1,)), ((), ())), preferred_element_type=jnp.float32
     ) * (1.0 / math.sqrt(HD))
     top = jnp.max(scores, axis=1, keepdims=True)
     weights = jnp.exp(scores - top)
-    total = jnp.sum(weights, axis=1, keepdims=True)
-    mixed = jnp.dot(weights.astype(jnp.bfloat16), v, preferred_element_type=jnp.float32)
-    return (mixed / total).astype(jnp.bfloat16)
+    return weights.astype(jnp.bfloat16), 1.0 / jnp.sum(weights, axis=1, keepdims=True)
+
+
+def mix(weights, scale, v):
+    mixed = jnp.dot(weights, v, preferred_element_type=jnp.float32)
+    return (mixed * scale).astype(jnp.bfloat16)
 
 
 def exchange_kernel(
     blks, teams, cores, whole, rest,
     q_ref, k_ref, v_ref, out_ref,
-    qw, kw, vw, ow, qr, kvr, orest,
+    qw, kw, vw, ow, weights, qr, kvr, orest,
     send_sem, out_send_sem, recv_sem, direct_sem, passed_sem, rest_q_sem, out_sem,
 ):
     rows = q_ref.shape[0]
@@ -164,18 +167,15 @@
                         device_id_type=MESH,
                     ).start()
 
-    for a, ref in enumerate((kw, qw, vw)):
+    for a, ref in enumerate((kw, qw)):
         arrived(ref, recv_sem.at[a])
-    chunk = 2 if members % 2 == 0 else 1
-    for g in range(whole):
-        for c in range(0, members, chunk):
-            span = pl.ds(c * rows, chunk * rows)
-            ow[g, span, :] = attend(qw[g, span, :], kw[g], vw[g])
-            for b in range(c, c + chunk):
-                put(
-                    ow.at[g, pl.ds(b * rows, rows), :], out_ref.at[:, head_cols(me * whole + g)],
-                    b == me, where(b), out_send_sem, out_sem,
-                )
+    half = members // 2 * rows
+    spans = (slice(0, half), slice(half, members * rows)) if half else (slice(0, rows),)
+    scales = []
+    for g in range(whole):
+        for span in spans:
+            weights[g, span, :], scale = soften(qw[g, span, :], kw[g])
+            scales.append(scale)
     first = (team * cores + core) * rest
     if rest:
         @pl.when(blk // rest == core)
@@ -188,13 +188,23 @@
             arrived(kvr, passed_sem)
 
         arrived(qr, rest_q_sem)
-        orest[...] = attend(qr[...], kvr[0], kvr[1])
+        orest[...] = mix(*soften(qr[...], kvr[0]), kvr[1])
         for b in range(rest):
             put(
                 orest.at[pl.ds(b * rows, rows), :],
                 out_ref.at[:, head_cols(members * whole + blk % rest)],
                 (blk // rest == core) & (first + b == me),
                 where(first + b, blk // rest), out_send_sem, out_sem,
+            )
+    arrived(vw, recv_sem.at[2])
+    for g in range(whole):
+        for span in spans:
+            ow[g, span, :] = mix(weights[g, span, :], scales.pop(0), vw[g])
+    for g in range(whole):
+        for b in range(members):
+            put(
+                ow.at[g, pl.ds(b * rows, rows), :], out_ref.at[:, head_cols(me * whole + g)],
+                b == me, where(b), out_send_sem, out_sem,
             )
 
     for copy in sent:
@@ -240,6 +250,7 @@
         out_specs=pl.BlockSpec(memory_space=pl.ANY),
         scratch_shapes=[
             full, full, full, full,
+            pltpu.VMEM((whole, members * rows, members * rows), bf16),
             rest_part, pltpu.VMEM((2, members * rows, HD), bf16), rest_part,
             pltpu.SemaphoreType.DMA,
             pltpu.SemaphoreType.DMA,

time: 22.7 us -> 22.3 us (0.982)
  no operation moved by 1% of the time
where the time goes in v3:
time: 22.3 us; the launch traced here: 22.1 us
  Pallas kernels  20.6 us (92%)
  local copies, waits for them, and re-layouts  1.56 us (7%)
    pallas_call x1, Pallas kernels, exchanged(): pl.pallas_call(partial(exchange_kernel, blks, teams, cores, whole, rest),...  20.6 us
    unnamed x1, local copies, waits for them, and re-layouts  1.56 us

profile of v3, /device:TPU:0, one launch (start us, length us, event | category | flops | bytes accessed | tf_op | source)
XLA Modules:
  0.0 22.1 jit_solution(18134092563672077882)
XLA Ops:
  0.0 20.6 %shard_map.37 = bf16[48,1280]{1,0:T(8,128)(2,1)} custom-call(bf16[48,1280]{1,0:T(8,128)(2,1)} %q_ref.1, bf16[48,1280]{1,0:T(8,128)(2,1)} %k_ref.1, bf16[48,1280]{1,0:T(8,128)(2,1)} %v_ref.1), custom_call_target="tpu_custom_call" | custom-call | tf_op jit(solution)/shard_map/pallas_call | solution.py:246
  20.6 1.6 %copy.5 = bf16[48,1280]{1,0:T(8,128)(2,1)} copy(bf16[48,1280]{1,0:T(8,128)(2,1)} %shard_map.37) | data formatting | bytes 245760

commit v4 on v3

--- a/solution.py
+++ b/solution.py
@@ -76,8 +76,8 @@
 def exchange_kernel(
     blks, teams, cores, whole, rest,
     q_ref, k_ref, v_ref, out_ref,
-    qw, kw, vw, ow, weights, qr, kvr, orest,
-    send_sem, out_send_sem, recv_sem, direct_sem, passed_sem, rest_q_sem, out_sem,
+    held, got, ow, weights, qr, kvr, orest,
+    load_sem, send_sem, out_send_sem, recv_sem, direct_sem, passed_sem, rest_q_sem, out_sem,
 ):
     rows = q_ref.shape[0]
     members = blks * teams
@@ -104,11 +104,18 @@
             pl.semaphore_signal(
                 barrier, inc=1, device_id=where(other, on_core), device_id_type=MESH
             )
-    for g in range(whole):
-        for a, (src, dst) in enumerate(((k_ref, kw), (q_ref, qw), (v_ref, vw))):
-            pltpu.make_async_copy(
-                src.at[:, head_cols(me * whole + g)], dst.at[g, at_rows(me), :], recv_sem.at[a]
-            ).start()
+    loads = [
+        pltpu.make_async_copy(src, held.at[a], load_sem.at[a])
+        for a, src in enumerate((q_ref, k_ref, v_ref))
+    ]
+    for load in loads:
+        load.start()
+    for load in loads:
+        load.wait()
+    for g in range(whole):
+        cols = head_cols(me * whole + g)
+        for a in range(3):
+            got[g, a, at_rows(me), :] = held[a, :, cols]
     pl.semaphore_wait(barrier, members * greeted - 1)
 
     def put(src, dst, here, device, sends, sem):
@@ -130,23 +137,22 @@
     for r in range(rest):
         home = core * rest + r
         cols = head_cols(members * whole + r)
-        for a, src in enumerate((k_ref, v_ref)):
-            put(
-                src.at[:, cols], kvr.at[a, at_rows(me), :], home == blk,
-                where(home * teams + team), send_sem, direct_sem.at[blk],
-            )
         put(
-            q_ref.at[:, cols], qr.at[at_rows(slot), :],
+            held.at[pl.ds(1, 2), :, cols], kvr.at[:, at_rows(me), :], home == blk,
+            where(home * teams + team), send_sem, direct_sem.at[blk],
+        )
+        put(
+            held.at[0, :, cols], qr.at[at_rows(slot), :],
             (home == blk) & (part == team * cores + core),
             where(home * teams + part // cores, part % cores), send_sem, rest_q_sem,
         )
     sent = []
-    for a, (src, dst) in enumerate(((k_ref, kw), (q_ref, qw), (v_ref, vw))):
+    for a, kinds in enumerate((pl.ds(0, 2), pl.ds(2, 1))):
         for other in others:
             for g in range(whole):
                 copy = pltpu.make_async_remote_copy(
-                    src_ref=src.at[:, head_cols(other * whole + g)],
-                    dst_ref=dst.at[g, at_rows(me), :],
+                    src_ref=held.at[kinds, :, head_cols(other * whole + g)],
+                    dst_ref=got.at[g, kinds, at_rows(me), :],
                     send_sem=send_sem, recv_sem=recv_sem.at[a],
                     device_id=where(other), device_id_type=MESH,
                 )
@@ -167,14 +173,14 @@
                         device_id_type=MESH,
                     ).start()
 
-    for a, ref in enumerate((kw, qw)):
-        arrived(ref, recv_sem.at[a])
+    far = pl.ds(0, (members - 1) * rows)
+    arrived(got.at[:, pl.ds(0, 2), far, :], recv_sem.at[0])
     half = members // 2 * rows
     spans = (slice(0, half), slice(half, members * rows)) if half else (slice(0, rows),)
     scales = []
     for g in range(whole):
         for span in spans:
-            weights[g, span, :], scale = soften(qw[g, span, :], kw[g])
+            weights[g, span, :], scale = soften(got[g, 0, span, :], got[g, 1])
             scales.append(scale)
     first = (team * cores + core) * rest
     if rest:
@@ -196,10 +202,10 @@
                 (blk // rest == core) & (first + b == me),
                 where(first + b, blk // rest), out_send_sem, out_sem,
             )
-    arrived(vw, recv_sem.at[2])
+    arrived(got.at[:, pl.ds(2, 1), far, :], recv_sem.at[1])
     for g in range(whole):
         for span in spans:
-            ow[g, span, :] = mix(weights[g, span, :], scales.pop(0), vw[g])
+            ow[g, span, :] = mix(weights[g, span, :], scales.pop(0), got[g, 2])
     for g in range(whole):
         for b in range(members):
             put(
@@ -215,8 +221,7 @@
 
         @pl.when(home != blk)
         def _():
-            for _ in range(2):
-                arrived(tile, send_sem)
+            arrived(kvr.at[:, pl.ds(0, rows), :], send_sem)
 
         @pl.when((home != blk) | (part != team * cores + core))
         def _():
@@ -241,7 +246,6 @@
     rows, columns = queries.shape
     members = blks * teams
     bf16 = jnp.bfloat16
-    full = pltpu.VMEM((whole, members * rows, HD), bf16)
     rest_part = pltpu.VMEM((max(rest, 1) * rows, HD), bf16)
     return pl.pallas_call(
         partial(exchange_kernel, blks, teams, cores, whole, rest),
@@ -249,12 +253,15 @@
         in_specs=[pl.BlockSpec(memory_space=pl.ANY)] * 3,
         out_specs=pl.BlockSpec(memory_space=pl.ANY),
         scratch_shapes=[
-            full, full, full, full,
+            pltpu.VMEM((3, rows, columns), bf16),
+            pltpu.VMEM((whole, 3, members * rows, HD), bf16),
+            pltpu.VMEM((whole, members * rows, HD), bf16),
             pltpu.VMEM((whole, members * rows, members * rows), bf16),
             rest_part, pltpu.VMEM((2, members * rows, HD), bf16), rest_part,
-            pltpu.SemaphoreType.DMA,
-            pltpu.SemaphoreType.DMA,
             pltpu.SemaphoreType.DMA((3,)),
+            pltpu.SemaphoreType.DMA,
+            pltpu.SemaphoreType.DMA,
+            pltpu.SemaphoreType.DMA((2,)),
             pltpu.SemaphoreType.DMA((blks,)),
             pltpu.SemaphoreType.DMA,
             pltpu.SemaphoreType.DMA,

time: 22.3 us -> 22 us (0.987)
  Pallas kernels: 20.6 us -> 20.3 us
    pallas_call x1, Pallas kernels: 20.6 us -> 20.3 us  [exchanged(): pl.pallas_call(partial(exchange_kernel, blks, teams, cores, whole, rest),...]
where the time goes in v4:
time: 22 us; the launch traced here: 21.9 us
  Pallas kernels  20.3 us (92%)
  local copies, waits for them, and re-layouts  1.56 us (7%)
    pallas_call x1, Pallas kernels, exchanged(): pl.pallas_call(partial(exchange_kernel, blks, teams, cores, whole, rest),...  20.3 us
    unnamed x1, local copies, waits for them, and re-layouts  1.56 us

profile of v4, /device:TPU:0, one launch (start us, length us, event | category | flops | bytes accessed | tf_op | source)
XLA Modules:
  0.0 21.9 jit_solution(12965637694136860120)
XLA Ops:
  0.0 20.3 %shard_map.37 = bf16[48,1280]{1,0:T(8,128)(2,1)} custom-call(bf16[48,1280]{1,0:T(8,128)(2,1)} %q_ref.1, bf16[48,1280]{1,0:T(8,128)(2,1)} %k_ref.1, bf16[48,1280]{1,0:T(8,128)(2,1)} %v_ref.1), custom_call_target="tpu_custom_call" | custom-call | tf_op jit(solution)/shard_map/pallas_call | solution.py:250
  20.3 1.6 %copy.5 = bf16[48,1280]{1,0:T(8,128)(2,1)} copy(bf16[48,1280]{1,0:T(8,128)(2,1)} %shard_map.37) | data formatting | bytes 245760

commit v5 on v4

--- a/solution.py
+++ b/solution.py
@@ -73,10 +73,18 @@
     return (mixed * scale).astype(jnp.bfloat16)
 
 
+def flipped(member, turn, members):
+    out, bit = 0, 1
+    while bit < members:
+        out = out + lax.rem(member // bit + turn // bit, 2) * bit
+        bit *= 2
+    return out
+
+
 def exchange_kernel(
     blks, teams, cores, whole, rest,
     q_ref, k_ref, v_ref, out_ref,
-    held, got, ow, weights, qr, kvr, orest,
+    held, got, ow, qr, kvr, orest,
     load_sem, send_sem, out_send_sem, recv_sem, direct_sem, passed_sem, rest_q_sem, out_sem,
 ):
     rows = q_ref.shape[0]
@@ -93,8 +101,12 @@
     def head_cols(head):
         return pl.ds(pl.multiple_of(head * HD, HD), HD)
 
-    steps = sorted(range(1, members), key=lambda s: -min(s, members - s))
-    others = [lax.rem(me + s, members) for s in steps]
+    if members & (members - 1) == 0:
+        others = sources = [flipped(me, s, members) for s in range(members - 1, 0, -1)]
+    else:
+        steps = sorted(range(1, members), key=lambda s: -min(s, members - s))
+        others = [lax.rem(me + s, members) for s in steps]
+        sources = [lax.rem(me + members - s, members) for s in steps]
 
     barrier = pltpu.get_barrier_semaphore()
     greeted = cores if rest else 1
@@ -115,7 +127,7 @@
     for g in range(whole):
         cols = head_cols(me * whole + g)
         for a in range(3):
-            got[g, a, at_rows(me), :] = held[a, :, cols]
+            got[g, a, pl.ds((members - 1) * rows, rows), :] = held[a, :, cols]
     pl.semaphore_wait(barrier, members * greeted - 1)
 
     def put(src, dst, here, device, sends, sem):
@@ -147,17 +159,26 @@
             where(home * teams + part // cores, part % cores), send_sem, rest_q_sem,
         )
     sent = []
-    for a, kinds in enumerate((pl.ds(0, 2), pl.ds(2, 1))):
-        for other in others:
+    far, last = members // 2, members - 1
+    all_heads = pl.ds(0, whole)
+    legs = ((0, 2, 0, far), (1, 2, far, last), (2, 3, 0, last), (0, 1, far, last))
+    for leg, (low, high, start, stop) in enumerate(legs):
+        for i in range(start, stop):
             for g in range(whole):
                 copy = pltpu.make_async_remote_copy(
-                    src_ref=held.at[kinds, :, head_cols(other * whole + g)],
-                    dst_ref=got.at[g, kinds, at_rows(me), :],
-                    send_sem=send_sem, recv_sem=recv_sem.at[a],
-                    device_id=where(other), device_id_type=MESH,
+                    src_ref=held.at[pl.ds(low, high - low), :, head_cols(others[i] * whole + g)],
+                    dst_ref=got.at[g, pl.ds(low, high - low), pl.ds(i * rows, rows), :],
+                    send_sem=send_sem, recv_sem=recv_sem.at[leg],
+                    device_id=where(others[i]), device_id_type=MESH,
                 )
                 copy.start()
                 sent.append(copy)
+
+    def leg_arrived(leg):
+        low, high, start, stop = legs[leg]
+        if stop > start:
+            span = pl.ds(start * rows, (stop - start) * rows)
+            arrived(got.at[all_heads, pl.ds(low, high - low), span, :], recv_sem.at[leg])
 
     if rest:
         @pl.when(blk // rest == core)
@@ -173,15 +194,6 @@
                         device_id_type=MESH,
                     ).start()
 
-    far = pl.ds(0, (members - 1) * rows)
-    arrived(got.at[:, pl.ds(0, 2), far, :], recv_sem.at[0])
-    half = members // 2 * rows
-    spans = (slice(0, half), slice(half, members * rows)) if half else (slice(0, rows),)
-    scales = []
-    for g in range(whole):
-        for span in spans:
-            weights[g, span, :], scale = soften(got[g, 0, span, :], got[g, 1])
-            scales.append(scale)
     first = (team * cores + core) * rest
     if rest:
         @pl.when(blk // rest == core)
@@ -202,16 +214,32 @@
                 (blk // rest == core) & (first + b == me),
                 where(first + b, blk // rest), out_send_sem, out_sem,
             )
-    arrived(got.at[:, pl.ds(2, 1), far, :], recv_sem.at[1])
+
+    def soften_slots(g, start, stop):
+        return soften(got[g, 0, pl.ds(start * rows, (stop - start) * rows), :], got[g, 1])
+
+    def give_slots(g, start, stop, weights, scale):
+        ow[g, pl.ds(start * rows, (stop - start) * rows), :] = mix(weights, scale, got[g, 2])
+        for i in range(start, stop):
+            src = ow.at[g, pl.ds(i * rows, rows), :]
+            dst = out_ref.at[:, head_cols(me * whole + g)]
+            if i == last:
+                pltpu.make_async_copy(src, dst, out_sem).start()
+            else:
+                pltpu.make_async_remote_copy(
+                    src_ref=src, dst_ref=dst, send_sem=out_send_sem, recv_sem=out_sem,
+                    device_id=where(sources[i]), device_id_type=MESH,
+                ).start()
+
+    leg_arrived(0)
+    leg_arrived(1)
+    softened = [soften_slots(g, 0, far) for g in range(whole)]
+    leg_arrived(2)
     for g in range(whole):
-        for span in spans:
-            ow[g, span, :] = mix(weights[g, span, :], scales.pop(0), got[g, 2])
+        give_slots(g, 0, far, *softened[g])
+    leg_arrived(3)
     for g in range(whole):
-        for b in range(members):
-            put(
-                ow.at[g, pl.ds(b * rows, rows), :], out_ref.at[:, head_cols(me * whole + g)],
-                b == me, where(b), out_send_sem, out_sem,
-            )
+        give_slots(g, far, members, *soften_slots(g, far, members))
 
     for copy in sent:
         copy.wait_send()
@@ -231,10 +259,7 @@
         def _():
             for _ in range(teams * cores - 1):
                 arrived(kvr.at[:, pl.ds(0, blks * rows), :], send_sem)
-    for b in range(members):
-        @pl.when(b != me)
-        def _():
-            arrived(ow.at[:, pl.ds(0, rows), :], out_send_sem)
+    arrived(ow.at[:, pl.ds(0, last * rows), :], out_send_sem)
     for b in range(rest):
         @pl.when((blk // rest != core) | (first + b != me))
         def _():
@@ -256,12 +281,11 @@
             pltpu.VMEM((3, rows, columns), bf16),
             pltpu.VMEM((whole, 3, members * rows, HD), bf16),
             pltpu.VMEM((whole, members * rows, HD), bf16),
-            pltpu.VMEM((whole, members * rows, members * rows), bf16),
             rest_part, pltpu.VMEM((2, members * rows, HD), bf16), rest_part,
             pltpu.SemaphoreType.DMA((3,)),
             pltpu.SemaphoreType.DMA,
             pltpu.SemaphoreType.DMA,
-            pltpu.SemaphoreType.DMA((2,)),
+            pltpu.SemaphoreType.DMA((4,)),
             pltpu.SemaphoreType.DMA((blks,)),
             pltpu.SemaphoreType.DMA,
             pltpu.SemaphoreType.DMA,
@@ -277,7 +301,7 @@
     def local(queries, key_rows, value_rows):
         heads = queries.shape[1] // HD
         whole, rest = heads // (blks * teams), heads % (blks * teams)
-        if whole >= 1 and rest * cores in (0, blks):
+        if whole >= 1 and blks * teams >= 2 and rest * cores in (0, blks):
             return exchanged(
                 queries, key_rows, value_rows,
                 blks=blks, teams=teams, cores=cores, whole=whole, rest=rest,

time: 22 us -> 22.7 us (1.032)
  Pallas kernels: 20.3 us -> 20.9 us
    pallas_call x1, Pallas kernels: 20.3 us -> 20.9 us  [exchanged(): pl.pallas_call(partial(exchange_kernel, blks, teams, cores, whole, rest),...]
where the time goes in v5:
time: 22.7 us; the launch traced here: 22.5 us
  Pallas kernels  20.9 us (92%)
  local copies, waits for them, and re-layouts  1.56 us (7%)
    pallas_call x1, Pallas kernels, exchanged(): pl.pallas_call(partial(exchange_kernel, blks, teams, cores, whole, rest),...  20.9 us
    unnamed x1, local copies, waits for them, and re-layouts  1.56 us

profile of v5, /device:TPU:0, one launch (start us, length us, event | category | flops | bytes accessed | tf_op | source)
XLA Modules:
  0.0 22.5 jit_solution(8352236673769668820)
XLA Ops:
  0.0 20.9 %shard_map.37 = bf16[48,1280]{1,0:T(8,128)(2,1)} custom-call(bf16[48,1280]{1,0:T(8,128)(2,1)} %q_ref.1, bf16[48,1280]{1,0:T(8,128)(2,1)} %k_ref.1, bf16[48,1280]{1,0:T(8,128)(2,1)} %v_ref.1), custom_call_target="tpu_custom_call" | custom-call | tf_op jit(solution)/shard_map/pallas_call | solution.py:275
  21.0 1.6 %copy.5 = bf16[48,1280]{1,0:T(8,128)(2,1)} copy(bf16[48,1280]{1,0:T(8,128)(2,1)} %shard_map.37) | data formatting | bytes 245760

commit v6 on v5

--- a/solution.py
+++ b/solution.py
@@ -159,27 +159,26 @@
             where(home * teams + part // cores, part % cores), send_sem, rest_q_sem,
         )
     sent = []
-    far, last = members // 2, members - 1
+    last = members - 1
     all_heads = pl.ds(0, whole)
-    legs = ((0, 2, 0, far), (1, 2, far, last), (2, 3, 0, last), (0, 1, far, last))
-    for leg, (low, high, start, stop) in enumerate(legs):
-        for i in range(start, stop):
+
+    def send_leg(leg, kinds):
+        for i in range(last):
             for g in range(whole):
                 copy = pltpu.make_async_remote_copy(
-                    src_ref=held.at[pl.ds(low, high - low), :, head_cols(others[i] * whole + g)],
-                    dst_ref=got.at[g, pl.ds(low, high - low), pl.ds(i * rows, rows), :],
+                    src_ref=held.at[kinds, :, head_cols(others[i] * whole + g)],
+                    dst_ref=got.at[g, kinds, pl.ds(i * rows, rows), :],
                     send_sem=send_sem, recv_sem=recv_sem.at[leg],
                     device_id=where(others[i]), device_id_type=MESH,
                 )
                 copy.start()
                 sent.append(copy)
 
-    def leg_arrived(leg):
-        low, high, start, stop = legs[leg]
-        if stop > start:
-            span = pl.ds(start * rows, (stop - start) * rows)
-            arrived(got.at[all_heads, pl.ds(low, high - low), span, :], recv_sem.at[leg])
-
+    def leg_arrived(leg, kinds):
+        arrived(got.at[all_heads, kinds, pl.ds(0, last * rows), :], recv_sem.at[leg])
+
+    queries_keys, values = pl.ds(0, 2), pl.ds(2, 1)
+    send_leg(0, queries_keys)
     if rest:
         @pl.when(blk // rest == core)
         def _():
@@ -194,6 +193,14 @@
                         device_id_type=MESH,
                     ).start()
 
+    send_leg(1, values)
+
+    leg_arrived(0, queries_keys)
+    half = members // 2 * rows
+    softened = [
+        [soften(got[g, 0, span, :], got[g, 1]) for span in (slice(0, half), slice(half, members * rows))]
+        for g in range(whole)
+    ]
     first = (team * cores + core) * rest
     if rest:
         @pl.when(blk // rest == core)
@@ -215,12 +222,12 @@
                 where(first + b, blk // rest), out_send_sem, out_sem,
             )
 
-    def soften_slots(g, start, stop):
-        return soften(got[g, 0, pl.ds(start * rows, (stop - start) * rows), :], got[g, 1])
-
-    def give_slots(g, start, stop, weights, scale):
-        ow[g, pl.ds(start * rows, (stop - start) * rows), :] = mix(weights, scale, got[g, 2])
-        for i in range(start, stop):
+    leg_arrived(1, values)
+    for g in range(whole):
+        for start, (weights, scale) in zip((0, half), softened[g]):
+            ow[g, pl.ds(start, weights.shape[0]), :] = mix(weights, scale, got[g, 2])
+    for g in range(whole):
+        for i in range(members):
             src = ow.at[g, pl.ds(i * rows, rows), :]
             dst = out_ref.at[:, head_cols(me * whole + g)]
             if i == last:
@@ -230,16 +237,6 @@
                     src_ref=src, dst_ref=dst, send_sem=out_send_sem, recv_sem=out_sem,
                     device_id=where(sources[i]), device_id_type=MESH,
                 ).start()
-
-    leg_arrived(0)
-    leg_arrived(1)
-    softened = [soften_slots(g, 0, far) for g in range(whole)]
-    leg_arrived(2)
-    for g in range(whole):
-        give_slots(g, 0, far, *softened[g])
-    leg_arrived(3)
-    for g in range(whole):
-        give_slots(g, far, members, *soften_slots(g, far, members))
 
     for copy in sent:
         copy.wait_send()
@@ -285,7 +282,7 @@
             pltpu.SemaphoreType.DMA((3,)),
             pltpu.SemaphoreType.DMA,
             pltpu.SemaphoreType.DMA,
-            pltpu.SemaphoreType.DMA((4,)),
+            pltpu.SemaphoreType.DMA((2,)),
             pltpu.SemaphoreType.DMA((blks,)),
             pltpu.SemaphoreType.DMA,
             pltpu.SemaphoreType.DMA,

time: 22.7 us -> 22.4 us (0.987)
    pallas_call x1, Pallas kernels: 20.9 us -> 20.7 us  [exchanged(): pl.pallas_call(partial(exchange_kernel, blks, teams, cores, whole, rest),...]
where the time goes in v6:
time: 22.4 us; the launch traced here: 22.3 us
  Pallas kernels  20.7 us (92%)
  local copies, waits for them, and re-layouts  1.56 us (7%)
    pallas_call x1, Pallas kernels, exchanged(): pl.pallas_call(partial(exchange_kernel, blks, teams, cores, whole, rest),...  20.7 us
    unnamed x1, local copies, waits for them, and re-layouts  1.56 us

profile of v6, /device:TPU:0, one launch (start us, length us, event | category | flops | bytes accessed | tf_op | source)
XLA Modules:
  0.0 22.3 jit_solution(17202264361808126346)
XLA Ops:
  0.0 20.7 %shard_map.37 = bf16[48,1280]{1,0:T(8,128)(2,1)} custom-call(bf16[48,1280]{1,0:T(8,128)(2,1)} %q_ref.1, bf16[48,1280]{1,0:T(8,128)(2,1)} %k_ref.1, bf16[48,1280]{1,0:T(8,128)(2,1)} %v_ref.1), custom_call_target="tpu_custom_call" | custom-call | tf_op jit(solution)/shard_map/pallas_call | solution.py:272
  20.7 1.6 %copy.5 = bf16[48,1280]{1,0:T(8,128)(2,1)} copy(bf16[48,1280]{1,0:T(8,128)(2,1)} %shard_map.37) | data formatting | bytes 245760

commit v7 on v6

--- a/solution.py
+++ b/solution.py
@@ -84,8 +84,8 @@
 def exchange_kernel(
     blks, teams, cores, whole, rest,
     q_ref, k_ref, v_ref, out_ref,
-    held, got, ow, qr, kvr, orest,
-    load_sem, send_sem, out_send_sem, recv_sem, direct_sem, passed_sem, rest_q_sem, out_sem,
+    held, got, ow, shared, orest,
+    load_sem, send_sem, out_send_sem, recv_sem, direct_sem, passed_sem, out_sem,
 ):
     rows = q_ref.shape[0]
     members = blks * teams
@@ -108,14 +108,28 @@
         others = [lax.rem(me + s, members) for s in steps]
         sources = [lax.rem(me + members - s, members) for s in steps]
 
+    helper, owner = cores - 1, (blk // rest if rest else 0)
+
     barrier = pltpu.get_barrier_semaphore()
-    greeted = cores if rest else 1
-    for turn in range(greeted):
-        on_core = lax.rem(core + turn, cores)
-        for other in others + ([me] if turn else []):
-            pl.semaphore_signal(
-                barrier, inc=1, device_id=where(other, on_core), device_id_type=MESH
-            )
+
+    def greet(member, on_core):
+        pl.semaphore_signal(
+            barrier, inc=1, device_id=where(member, on_core), device_id_type=MESH
+        )
+
+    for other in others:
+        greet(other, core)
+    if rest and cores > 1:
+        @pl.when(core != helper)
+        def _():
+            for r in range(rest):
+                greet((core * rest + r) * teams + team, helper)
+
+        @pl.when((core == helper) & (owner != helper))
+        def _():
+            for b in range(blks):
+                greet(b * teams + team, owner)
+
     loads = [
         pltpu.make_async_copy(src, held.at[a], load_sem.at[a])
         for a, src in enumerate((q_ref, k_ref, v_ref))
@@ -128,7 +142,10 @@
         cols = head_cols(me * whole + g)
         for a in range(3):
             got[g, a, pl.ds((members - 1) * rows, rows), :] = held[a, :, cols]
-    pl.semaphore_wait(barrier, members * greeted - 1)
+    greeted = members - 1
+    if rest and cores > 1:
+        greeted = greeted + jnp.where(core != helper, rest, jnp.where(owner != helper, blks, 0))
+    pl.semaphore_wait(barrier, greeted)
 
     def put(src, dst, here, device, sends, sem):
         @pl.when(here)
@@ -145,18 +162,12 @@
     def arrived(ref, sem):
         pltpu.make_async_copy(ref, ref, sem).wait()
 
-    part, slot = (me // rest, me % rest) if rest else (0, 0)
     for r in range(rest):
         home = core * rest + r
-        cols = head_cols(members * whole + r)
         put(
-            held.at[pl.ds(1, 2), :, cols], kvr.at[:, at_rows(me), :], home == blk,
-            where(home * teams + team), send_sem, direct_sem.at[blk],
-        )
-        put(
-            held.at[0, :, cols], qr.at[at_rows(slot), :],
-            (home == blk) & (part == team * cores + core),
-            where(home * teams + part // cores, part % cores), send_sem, rest_q_sem,
+            held.at[:, :, head_cols(members * whole + r)], shared.at[:, at_rows(blk), :],
+            (home == blk) & (core == helper), where(home * teams + team, helper),
+            send_sem, direct_sem.at[blk],
         )
     sent = []
     last = members - 1
@@ -177,19 +188,19 @@
     def leg_arrived(leg, kinds):
         arrived(got.at[all_heads, kinds, pl.ds(0, last * rows), :], recv_sem.at[leg])
 
-    queries_keys, values = pl.ds(0, 2), pl.ds(2, 1)
+    queries_keys, keys_values, values = pl.ds(0, 2), pl.ds(1, 2), pl.ds(2, 1)
     send_leg(0, queries_keys)
     if rest:
-        @pl.when(blk // rest == core)
+        @pl.when(core == helper)
         def _():
             for b in range(blks):
-                block = kvr.at[:, at_rows(b * teams + team), :]
-                arrived(block, direct_sem.at[b])
-                for turn in range(1, teams * cores):
-                    t = lax.rem(team + turn // cores, teams)
+                arrived(shared.at[:, pl.ds(b * rows, rows), :], direct_sem.at[b])
+                for turn in range(1, teams):
                     pltpu.make_async_remote_copy(
-                        src_ref=block, dst_ref=block, send_sem=send_sem, recv_sem=passed_sem,
-                        device_id=where(blk * teams + t, lax.rem(core + turn % cores, cores)),
+                        src_ref=shared.at[keys_values, pl.ds(b * rows, rows), :],
+                        dst_ref=shared.at[keys_values, pl.ds((turn * blks + b) * rows, rows), :],
+                        send_sem=send_sem, recv_sem=passed_sem,
+                        device_id=where(blk * teams + lax.rem(team + turn, teams)),
                         device_id_type=MESH,
                     ).start()
 
@@ -201,26 +212,21 @@
         [soften(got[g, 0, span, :], got[g, 1]) for span in (slice(0, half), slice(half, members * rows))]
         for g in range(whole)
     ]
-    first = (team * cores + core) * rest
+    passed = shared.at[keys_values, pl.ds(0, (teams - 1) * blks * rows), :]
     if rest:
-        @pl.when(blk // rest == core)
+        @pl.when(core == helper)
         def _():
             if teams > 1:
-                arrived(kvr.at[:, pl.ds(0, (teams - 1) * blks * rows), :], passed_sem)
-
-        @pl.when(blk // rest != core)
-        def _():
-            arrived(kvr, passed_sem)
-
-        arrived(qr, rest_q_sem)
-        orest[...] = mix(*soften(qr[...], kvr[0]), kvr[1])
-        for b in range(rest):
-            put(
-                orest.at[pl.ds(b * rows, rows), :],
-                out_ref.at[:, head_cols(members * whole + blk % rest)],
-                (blk // rest == core) & (first + b == me),
-                where(first + b, blk // rest), out_send_sem, out_sem,
-            )
+                arrived(passed, passed_sem)
+            mine = shared[0, pl.ds(0, blks * rows), :]
+            orest[...] = mix(*soften(mine, shared[1]), shared[2])
+            for b in range(blks):
+                put(
+                    orest.at[pl.ds(b * rows, rows), :],
+                    out_ref.at[:, head_cols(members * whole + blk % rest)],
+                    (owner == helper) & (b == blk), where(b * teams + team, owner),
+                    out_send_sem, out_sem,
+                )
 
     leg_arrived(1, values)
     for g in range(whole):
@@ -240,27 +246,20 @@
 
     for copy in sent:
         copy.wait_send()
-    tile = ow.at[0, pl.ds(0, rows), :]
     for r in range(rest):
-        home = core * rest + r
-
-        @pl.when(home != blk)
-        def _():
-            arrived(kvr.at[:, pl.ds(0, rows), :], send_sem)
-
-        @pl.when((home != blk) | (part != team * cores + core))
-        def _():
-            arrived(tile, send_sem)
+        @pl.when((core * rest + r != blk) | (core != helper))
+        def _():
+            arrived(shared.at[:, pl.ds(0, rows), :], send_sem)
+    arrived(ow.at[:, pl.ds(0, last * rows), :], out_send_sem)
     if rest:
-        @pl.when(blk // rest == core)
-        def _():
-            for _ in range(teams * cores - 1):
-                arrived(kvr.at[:, pl.ds(0, blks * rows), :], send_sem)
-    arrived(ow.at[:, pl.ds(0, last * rows), :], out_send_sem)
-    for b in range(rest):
-        @pl.when((blk // rest != core) | (first + b != me))
-        def _():
-            arrived(tile, out_send_sem)
+        @pl.when(core == helper)
+        def _():
+            if teams > 1:
+                arrived(passed, send_sem)
+            for b in range(blks):
+                @pl.when((owner != helper) | (b != blk))
+                def _():
+                    arrived(orest.at[pl.ds(b * rows, rows), :], out_send_sem)
     arrived(out_ref, out_sem)
 
 
@@ -268,7 +267,6 @@
     rows, columns = queries.shape
     members = blks * teams
     bf16 = jnp.bfloat16
-    rest_part = pltpu.VMEM((max(rest, 1) * rows, HD), bf16)
     return pl.pallas_call(
         partial(exchange_kernel, blks, teams, cores, whole, rest),
         out_shape=jax.ShapeDtypeStruct((rows, columns), bf16),
@@ -278,13 +276,13 @@
             pltpu.VMEM((3, rows, columns), bf16),
             pltpu.VMEM((whole, 3, members * rows, HD), bf16),
             pltpu.VMEM((whole, members * rows, HD), bf16),
-            rest_part, pltpu.VMEM((2, members * rows, HD), bf16), rest_part,
+            pltpu.VMEM((3, members * rows, HD), bf16),
+            pltpu.VMEM((blks * rows, HD), bf16),
             pltpu.SemaphoreType.DMA((3,)),
             pltpu.SemaphoreType.DMA,
             pltpu.SemaphoreType.DMA,
             pltpu.SemaphoreType.DMA((2,)),
             pltpu.SemaphoreType.DMA((blks,)),
-            pltpu.SemaphoreType.DMA,
             pltpu.SemaphoreType.DMA,
             pltpu.SemaphoreType.DMA,
         ],

time: 22.4 us -> 21.4 us (0.955)
  Pallas kernels: 20.7 us -> 19.6 us
    pallas_call x1, Pallas kernels: 20.7 us -> 19.6 us  [exchanged(): pl.pallas_call(partial(exchange_kernel, blks, teams, cores, whole, rest),...]
where the time goes in v7:
time: 21.4 us; the launch traced here: 21.2 us
  Pallas kernels  19.6 us (92%)
  local copies, waits for them, and re-layouts  1.56 us (7%)
    pallas_call x1, Pallas kernels, exchanged(): pl.pallas_call(partial(exchange_kernel, blks, teams, cores, whole, rest),...  19.6 us
    unnamed x1, local copies, waits for them, and re-layouts  1.56 us

profile of v7, /device:TPU:0, one launch (start us, length us, event | category | flops | bytes accessed | tf_op | source)
XLA Modules:
  0.0 21.2 jit_solution(16114063659798652869)
XLA Ops:
  0.0 19.6 %shard_map.37 = bf16[48,1280]{1,0:T(8,128)(2,1)} custom-call(bf16[48,1280]{1,0:T(8,128)(2,1)} %q_ref.1, bf16[48,1280]{1,0:T(8,128)(2,1)} %k_ref.1, bf16[48,1280]{1,0:T(8,128)(2,1)} %v_ref.1), custom_call_target="tpu_custom_call" | custom-call | tf_op jit(solution)/shard_map/pallas_call | solution.py:270
  19.7 1.6 %copy.5 = bf16[48,1280]{1,0:T(8,128)(2,1)} copy(bf16[48,1280]{1,0:T(8,128)(2,1)} %shard_map.37) | data formatting | bytes 245760

commit v8 on v7

--- a/solution.py
+++ b/solution.py
@@ -102,33 +102,12 @@
         return pl.ds(pl.multiple_of(head * HD, HD), HD)
 
     if members & (members - 1) == 0:
-        others = sources = [flipped(me, s, members) for s in range(members - 1, 0, -1)]
+        others = [flipped(me, s, members) for s in range(members - 1, 0, -1)]
     else:
         steps = sorted(range(1, members), key=lambda s: -min(s, members - s))
         others = [lax.rem(me + s, members) for s in steps]
-        sources = [lax.rem(me + members - s, members) for s in steps]
 
     helper, owner = cores - 1, (blk // rest if rest else 0)
-
-    barrier = pltpu.get_barrier_semaphore()
-
-    def greet(member, on_core):
-        pl.semaphore_signal(
-            barrier, inc=1, device_id=where(member, on_core), device_id_type=MESH
-        )
-
-    for other in others:
-        greet(other, core)
-    if rest and cores > 1:
-        @pl.when(core != helper)
-        def _():
-            for r in range(rest):
-                greet((core * rest + r) * teams + team, helper)
-
-        @pl.when((core == helper) & (owner != helper))
-        def _():
-            for b in range(blks):
-                greet(b * teams + team, owner)
 
     loads = [
         pltpu.make_async_copy(src, held.at[a], load_sem.at[a])
@@ -136,12 +115,28 @@
     ]
     for load in loads:
         load.start()
+    barrier = pltpu.get_barrier_semaphore()
+
+    def greet(member, on_core):
+        pl.semaphore_signal(
+            barrier, inc=1, device_id=where(member, on_core), device_id_type=MESH
+        )
+
+    for other in others:
+        greet(other, core)
+    if rest and cores > 1:
+        @pl.when(core != helper)
+        def _():
+            for r in range(rest):
+                greet((core * rest + r) * teams + team, helper)
+
+        @pl.when((core == helper) & (owner != helper))
+        def _():
+            for b in range(blks):
+                greet(b * teams + team, owner)
+
     for load in loads:
         load.wait()
-    for g in range(whole):
-        cols = head_cols(me * whole + g)
-        for a in range(3):
-            got[g, a, pl.ds((members - 1) * rows, rows), :] = held[a, :, cols]
     greeted = members - 1
     if rest and cores > 1:
         greeted = greeted + jnp.where(core != helper, rest, jnp.where(owner != helper, blks, 0))
@@ -178,7 +173,7 @@
             for g in range(whole):
                 copy = pltpu.make_async_remote_copy(
                     src_ref=held.at[kinds, :, head_cols(others[i] * whole + g)],
-                    dst_ref=got.at[g, kinds, pl.ds(i * rows, rows), :],
+                    dst_ref=got.at[g, kinds, at_rows(me), :],
                     send_sem=send_sem, recv_sem=recv_sem.at[leg],
                     device_id=where(others[i]), device_id_type=MESH,
                 )
@@ -206,6 +201,9 @@
 
     send_leg(1, values)
 
+    for g in range(whole):
+        for a in range(3):
+            got[g, a, at_rows(me), :] = held[a, :, head_cols(me * whole + g)]
     leg_arrived(0, queries_keys)
     half = members // 2 * rows
     softened = [
@@ -233,16 +231,11 @@
         for start, (weights, scale) in zip((0, half), softened[g]):
             ow[g, pl.ds(start, weights.shape[0]), :] = mix(weights, scale, got[g, 2])
     for g in range(whole):
-        for i in range(members):
-            src = ow.at[g, pl.ds(i * rows, rows), :]
-            dst = out_ref.at[:, head_cols(me * whole + g)]
-            if i == last:
-                pltpu.make_async_copy(src, dst, out_sem).start()
-            else:
-                pltpu.make_async_remote_copy(
-                    src_ref=src, dst_ref=dst, send_sem=out_send_sem, recv_sem=out_sem,
-                    device_id=where(sources[i]), device_id_type=MESH,
-                ).start()
+        for b in range(members):
+            put(
+                ow.at[g, pl.ds(b * rows, rows), :], out_ref.at[:, head_cols(me * whole + g)],
+                b == me, where(b), out_send_sem, out_sem,
+            )
 
     for copy in sent:
         copy.wait_send()

time: 21.4 us -> 21.5 us (level)
  no operation moved by 1% of the time
where the time goes in v8:
time: 21.5 us; the launch traced here: 21.3 us
  Pallas kernels  19.7 us (92%)
  local copies, waits for them, and re-layouts  1.56 us (7%)
    pallas_call x1, Pallas kernels, exchanged(): pl.pallas_call(partial(exchange_kernel, blks, teams, cores, whole, rest),...  19.7 us
    unnamed x1, local copies, waits for them, and re-layouts  1.56 us

profile of v8, /device:TPU:0, one launch (start us, length us, event | category | flops | bytes accessed | tf_op | source)
XLA Modules:
  0.0 21.3 jit_solution(7291077841675178731)
XLA Ops:
  0.0 19.7 %shard_map.37 = bf16[48,1280]{1,0:T(8,128)(2,1)} custom-call(bf16[48,1280]{1,0:T(8,128)(2,1)} %q_ref.1, bf16[48,1280]{1,0:T(8,128)(2,1)} %k_ref.1, bf16[48,1280]{1,0:T(8,128)(2,1)} %v_ref.1), custom_call_target="tpu_custom_call" | custom-call | tf_op jit(solution)/shard_map/pallas_call | solution.py:263
  19.7 1.6 %copy.5 = bf16[48,1280]{1,0:T(8,128)(2,1)} copy(bf16[48,1280]{1,0:T(8,128)(2,1)} %shard_map.37) | data formatting | bytes 245760

commit v9 on v8

--- a/solution.py
+++ b/solution.py
@@ -84,7 +84,7 @@
 def exchange_kernel(
     blks, teams, cores, whole, rest,
     q_ref, k_ref, v_ref, out_ref,
-    held, got, ow, shared, orest,
+    staged, held, got, ow, shared, orest,
     load_sem, send_sem, out_send_sem, recv_sem, direct_sem, passed_sem, out_sem,
 ):
     rows = q_ref.shape[0]
@@ -110,7 +110,7 @@
     helper, owner = cores - 1, (blk // rest if rest else 0)
 
     loads = [
-        pltpu.make_async_copy(src, held.at[a], load_sem.at[a])
+        pltpu.make_async_copy(src, staged.at[a], load_sem.at[a])
         for a, src in enumerate((q_ref, k_ref, v_ref))
     ]
     for load in loads:
@@ -135,8 +135,10 @@
             for b in range(blks):
                 greet(b * teams + team, owner)
 
-    for load in loads:
+    for a, load in enumerate(loads):
         load.wait()
+        for head in range(members * whole + rest):
+            held[head, a] = staged[a, :, pl.ds(head * HD, HD)]
     greeted = members - 1
     if rest and cores > 1:
         greeted = greeted + jnp.where(core != helper, rest, jnp.where(owner != helper, blks, 0))
@@ -160,7 +162,7 @@
     for r in range(rest):
         home = core * rest + r
         put(
-            held.at[:, :, head_cols(members * whole + r)], shared.at[:, at_rows(blk), :],
+            held.at[members * whole + r], shared.at[:, at_rows(blk), :],
             (home == blk) & (core == helper), where(home * teams + team, helper),
             send_sem, direct_sem.at[blk],
         )
@@ -172,7 +174,7 @@
         for i in range(last):
             for g in range(whole):
                 copy = pltpu.make_async_remote_copy(
-                    src_ref=held.at[kinds, :, head_cols(others[i] * whole + g)],
+                    src_ref=held.at[others[i] * whole + g, kinds],
                     dst_ref=got.at[g, kinds, at_rows(me), :],
                     send_sem=send_sem, recv_sem=recv_sem.at[leg],
                     device_id=where(others[i]), device_id_type=MESH,
@@ -203,7 +205,7 @@
 
     for g in range(whole):
         for a in range(3):
-            got[g, a, at_rows(me), :] = held[a, :, head_cols(me * whole + g)]
+            got[g, a, at_rows(me), :] = held[me * whole + g, a]
     leg_arrived(0, queries_keys)
     half = members // 2 * rows
     softened = [
@@ -267,6 +269,7 @@
         out_specs=pl.BlockSpec(memory_space=pl.ANY),
         scratch_shapes=[
             pltpu.VMEM((3, rows, columns), bf16),
+            pltpu.VMEM((columns // HD, 3, rows, HD), bf16),
             pltpu.VMEM((whole, 3, members * rows, HD), bf16),
             pltpu.VMEM((whole, members * rows, HD), bf16),
             pltpu.VMEM((3, members * rows, HD), bf16),

time: 21.5 us -> 21.5 us (level)
  no operation moved by 1% of the time
where the time goes in v9:
time: 21.5 us; the launch traced here: 21.3 us
  Pallas kernels  19.7 us (92%)
  local copies, waits for them, and re-layouts  1.56 us (7%)
    pallas_call x1, Pallas kernels, exchanged(): pl.pallas_call(partial(exchange_kernel, blks, teams, cores, whole, rest),...  19.7 us
    unnamed x1, local copies, waits for them, and re-layouts  1.56 us

profile of v9, /device:TPU:0, one launch (start us, length us, event | category | flops | bytes accessed | tf_op | source)
XLA Modules:
  0.0 21.3 jit_solution(8981191022833110731)
XLA Ops:
  0.0 19.7 %shard_map.37 = bf16[48,1280]{1,0:T(8,128)(2,1)} custom-call(bf16[48,1280]{1,0:T(8,128)(2,1)} %q_ref.1, bf16[48,1280]{1,0:T(8,128)(2,1)} %k_ref.1, bf16[48,1280]{1,0:T(8,128)(2,1)} %v_ref.1), custom_call_target="tpu_custom_call" | custom-call | tf_op jit(solution)/shard_map/pallas_call | solution.py:265
  19.7 1.6 %copy.5 = bf16[48,1280]{1,0:T(8,128)(2,1)} copy(bf16[48,1280]{1,0:T(8,128)(2,1)} %shard_map.37) | data formatting | bytes 245760

commit v10 on v9

--- a/solution.py
+++ b/solution.py
@@ -106,6 +106,9 @@
     else:
         steps = sorted(range(1, members), key=lambda s: -min(s, members - s))
         others = [lax.rem(me + s, members) for s in steps]
+    others = [
+        jnp.where(lax.rem(core, 2) == 0, near, far) for near, far in zip(reversed(others), others)
+    ]
 
     helper, owner = cores - 1, (blk // rest if rest else 0)
 

time: 21.5 us -> 21.3 us (level)
  no operation moved by 1% of the time
where the time goes in v10:
time: 21.3 us; the launch traced here: 21.2 us
  Pallas kernels  19.6 us (92%)
  local copies, waits for them, and re-layouts  1.56 us (7%)
    pallas_call x1, Pallas kernels, exchanged(): pl.pallas_call(partial(exchange_kernel, blks, teams, cores, whole, rest),...  19.6 us
    unnamed x1, local copies, waits for them, and re-layouts  1.56 us

profile of v10, /device:TPU:0, one launch (start us, length us, event | category | flops | bytes accessed | tf_op | source)
XLA Modules:
  0.0 21.2 jit_solution(9828311396176762574)
XLA Ops:
  0.0 19.6 %shard_map.37 = bf16[48,1280]{1,0:T(8,128)(2,1)} custom-call(bf16[48,1280]{1,0:T(8,128)(2,1)} %q_ref.1, bf16[48,1280]{1,0:T(8,128)(2,1)} %k_ref.1, bf16[48,1280]{1,0:T(8,128)(2,1)} %v_ref.1), custom_call_target="tpu_custom_call" | custom-call | tf_op jit(solution)/shard_map/pallas_call | solution.py:268
  19.6 1.6 %copy.5 = bf16[48,1280]{1,0:T(8,128)(2,1)} copy(bf16[48,1280]{1,0:T(8,128)(2,1)} %shard_map.37) | data formatting | bytes 245760

commit v11 on v9

--- a/solution.py
+++ b/solution.py
@@ -258,11 +258,37 @@
     arrived(out_ref, out_sem)
 
 
+def settle_kernel(pieces, src, dst, sem):
+    span = src.shape[0] // pieces
+    copies = [
+        pltpu.make_async_copy(
+            src.at[pl.ds(i * span, span), :], dst.at[pl.ds(i * span, span), :], sem.at[i]
+        )
+        for i in range(pieces)
+    ]
+    for copy in copies:
+        copy.start()
+    for copy in copies:
+        copy.wait()
+
+
+def settled(result):
+    rows = result.shape[0]
+    pieces = rows // 16 if rows % 16 == 0 else 1
+    return pl.pallas_call(
+        partial(settle_kernel, pieces),
+        out_shape=jax.ShapeDtypeStruct(result.shape, result.dtype),
+        in_specs=[pl.BlockSpec(memory_space=pl.ANY)],
+        out_specs=pl.BlockSpec(memory_space=pl.ANY),
+        scratch_shapes=[pltpu.SemaphoreType.DMA((pieces,))],
+    )(result)
+
+
 def exchanged(queries, key_rows, value_rows, *, blks, teams, cores, whole, rest):
     rows, columns = queries.shape
     members = blks * teams
     bf16 = jnp.bfloat16
-    return pl.pallas_call(
+    return settled(pl.pallas_call(
         partial(exchange_kernel, blks, teams, cores, whole, rest),
         out_shape=jax.ShapeDtypeStruct((rows, columns), bf16),
         in_specs=[pl.BlockSpec(memory_space=pl.ANY)] * 3,
@@ -283,7 +309,7 @@
             pltpu.SemaphoreType.DMA,
         ],
         compiler_params=pltpu.CompilerParams(collective_id=0, has_side_effects=True),
-    )(queries, key_rows, value_rows)
+    )(queries, key_rows, value_rows))
 
 
 def solution(mesh):

time: 21.5 us -> 24.7 us (1.15)
  Pallas kernels: 19.7 us -> 24.6 us
  local copies, waits for them, and re-layouts: 1.56 us -> 0 us
    pallas_call x0 -> x1, Pallas kernels: none -> 4.85 us  [settled(): pl.pallas_call(partial(settle_kernel, pieces), out_shape=jax.ShapeDtypeSt...]
    unnamed x1 -> x0, local copies, waits for them, and re-layouts: 1.56 us -> none
where the time goes in v11:
time: 24.7 us; the launch traced here: 24.6 us
  Pallas kernels  24.6 us (100%)
    pallas_call x1, Pallas kernels, exchanged(): pl.pallas_call(partial(exchange_kernel, blks, teams, cores, whole, rest),...  19.7 us
    pallas_call x1, Pallas kernels, settled(): pl.pallas_call(partial(settle_kernel, pieces), out_shape=jax.ShapeDtypeSt...  4.85 us

profile of v11, /device:TPU:0, one launch (start us, length us, event | category | flops | bytes accessed | tf_op | source)
XLA Modules:
  0.0 24.6 jit_solution(7855043839903352958)
XLA Ops:
  0.0 19.7 %shard_map.37.src = bf16[48,1280]{1,0:T(8,128)(2,1)} custom-call(bf16[48,1280]{1,0:T(8,128)(2,1)} %q_ref.1, bf16[48,1280]{1,0:T(8,128)(2,1)} %k_ref.1, bf16[48,1280]{1,0:T(8,128)(2,1)} %v_ref.1), custom_call_target="tpu_custom_call" | custom-call | tf_op jit(solution)/shard_map/pallas_call | solution.py:291
  19.7 4.9 %shard_map.38 = bf16[48,1280]{1,0:T(8,128)(2,1)} custom-call(bf16[48,1280]{1,0:T(8,128)(2,1)} %shard_map.37.src), custom_call_target="tpu_custom_call" | custom-call | tf_op jit(solution)/shard_map/pallas_call | solution.py:278

commit v12 on v9

--- a/solution.py
+++ b/solution.py
@@ -282,7 +282,9 @@
             pltpu.SemaphoreType.DMA,
             pltpu.SemaphoreType.DMA,
         ],
-        compiler_params=pltpu.CompilerParams(collective_id=0, has_side_effects=True),
+        compiler_params=pltpu.CompilerParams(
+            collective_id=0, has_side_effects=True, vmem_limit_bytes=16 * 3 * queries.size * queries.dtype.itemsize
+        ),
     )(queries, key_rows, value_rows)
 
 

time: 21.5 us -> 23.6 us (1.098)
  local copies, waits for them, and re-layouts: 1.56 us -> 3.35 us
  Pallas kernels: 19.7 us -> 20.1 us
    unnamed x1 -> x7, local copies, waits for them, and re-layouts: 1.56 us -> 3.35 us
    pallas_call x1, Pallas kernels: 19.7 us -> 20.1 us  [exchanged(): pl.pallas_call(partial(exchange_kernel, blks, teams, cores, whole, rest),...]
where the time goes in v12:
time: 23.6 us; the launch traced here: 23.4 us
  Pallas kernels  20.1 us (85%)
  local copies, waits for them, and re-layouts  3.35 us (14%)
    pallas_call x1, Pallas kernels, exchanged(): pl.pallas_call(partial(exchange_kernel, blks, teams, cores, whole, rest),...  20.1 us
    unnamed x7, local copies, waits for them, and re-layouts  3.35 us

profile of v12, /device:TPU:0, one launch (start us, length us, event | category | flops | bytes accessed | tf_op | source)
XLA Modules:
  0.0 23.4 jit_solution(11889055879078591008)
XLA Ops:
  0.0 0.0 copy-start
  0.0 0.9 %copy-done = bf16[48,1280]{1,0:T(8,128)(2,1)S(1)} copy-done((bf16[48,1280]{1,0:T(8,128)(2,1)S(1)}, bf16[48,1280]{1,0:T(8,128)(2,1)}, u32[]{:S(2)}) %copy-start) | copy-done | bytes 122904
  0.9 0.0 copy-start.1
  0.9 0.9 %copy-done.1 = bf16[48,1280]{1,0:T(8,128)(2,1)S(1)} copy-done((bf16[48,1280]{1,0:T(8,128)(2,1)S(1)}, bf16[48,1280]{1,0:T(8,128)(2,1)}, u32[]{:S(2)}) %copy-start.1) | copy-done | bytes 122904
  1.8 0.0 copy-start.2
  1.8 0.9 %copy-done.2 = bf16[48,1280]{1,0:T(8,128)(2,1)S(1)} copy-done((bf16[48,1280]{1,0:T(8,128)(2,1)S(1)}, bf16[48,1280]{1,0:T(8,128)(2,1)}, u32[]{:S(2)}) %copy-start.2) | copy-done | bytes 122904
  2.7 20.1 %shard_map.37 = bf16[48,1280]{1,0:T(8,128)(2,1)S(1)} custom-call(bf16[48,1280]{1,0:T(8,128)(2,1)S(1)} %copy-done, bf16[48,1280]{1,0:T(8,128)(2,1)S(1)} %copy-done.1, bf16[48,1280]{1,0:T(8,128)(2,1)S(1)} %copy-done.2), custom_call_target="tpu_custom_call" | custom-call | tf_op jit(solution)/shard_map/pallas_call | solution.py:265
  22.8 0.7 %copy.5 = bf16[48,1280]{1,0:T(8,128)(2,1)} copy(bf16[48,1280]{1,0:T(8,128)(2,1)S(1)} %shard_map.37) | data formatting | bytes 245760
Async XLA Ops:
  0.0 0.9 %copy-start = (bf16[48,1280]{1,0:T(8,128)(2,1)S(1)}, bf16[48,1280]{1,0:T(8,128)(2,1)}, u32[]{:S(2)}) copy-start(bf16[48,1280]{1,0:T(8,128)(2,1)} %q_ref.1) | copy-start | bytes 368644
  0.9 0.9 %copy-start.1 = (bf16[48,1280]{1,0:T(8,128)(2,1)S(1)}, bf16[48,1280]{1,0:T(8,128)(2,1)}, u32[]{:S(2)}) copy-start(bf16[48,1280]{1,0:T(8,128)(2,1)} %k_ref.1) | copy-start | bytes 368644
  1.8 0.9 %copy-start.2 = (bf16[48,1280]{1,0:T(8,128)(2,1)S(1)}, bf16[48,1280]{1,0:T(8,128)(2,1)}, u32[]{:S(2)}) copy-start(bf16[48,1280]{1,0:T(8,128)(2,1)} %v_ref.1) | copy-start | bytes 368644

commit v13 on v12

--- a/solution.py
+++ b/solution.py
@@ -264,7 +264,7 @@
     bf16 = jnp.bfloat16
     return pl.pallas_call(
         partial(exchange_kernel, blks, teams, cores, whole, rest),
-        out_shape=jax.ShapeDtypeStruct((rows, columns), bf16),
+        out_shape=pltpu.VMEM((rows, columns), bf16),
         in_specs=[pl.BlockSpec(memory_space=pl.ANY)] * 3,
         out_specs=pl.BlockSpec(memory_space=pl.ANY),
         scratch_shapes=[
@@ -285,7 +285,7 @@
         compiler_params=pltpu.CompilerParams(
             collective_id=0, has_side_effects=True, vmem_limit_bytes=16 * 3 * queries.size * queries.dtype.itemsize
         ),
-    )(queries, key_rows, value_rows)
+    )(*(pltpu.with_memory_space_constraint(x, pltpu.HBM) for x in (queries, key_rows, value_rows)))
 
 
 def solution(mesh):

time: 23.6 us -> 20.4 us (0.86)
  local copies, waits for them, and re-layouts: 3.35 us -> 0.65 us
  Pallas kernels: 20.1 us -> 19.6 us
    unnamed x7 -> x1, local copies, waits for them, and re-layouts: 3.35 us -> 0.65 us
    pallas_call x1, Pallas kernels: 20.1 us -> 19.6 us  [exchanged(): pl.pallas_call(partial(exchange_kernel, blks, teams, cores, whole, rest),...]
where the time goes in v13:
time: 20.4 us; the launch traced here: 20.3 us
  Pallas kernels  19.6 us (96%)
  local copies, waits for them, and re-layouts  0.65 us (3%)
    pallas_call x1, Pallas kernels, exchanged(): pl.pallas_call(partial(exchange_kernel, blks, teams, cores, whole, rest),...  19.6 us
    unnamed x1, local copies, waits for them, and re-layouts  0.65 us

profile of v13, /device:TPU:0, one launch (start us, length us, event | category | flops | bytes accessed | tf_op | source)
XLA Modules:
  0.0 20.3 jit_solution(5064993458609886942)
XLA Ops:
  0.0 19.6 %shard_map.37 = bf16[48,1280]{1,0:T(8,128)(2,1)S(1)} custom-call(bf16[48,1280]{1,0:T(8,128)(2,1)} %q_ref.1, bf16[48,1280]{1,0:T(8,128)(2,1)} %k_ref.1, bf16[48,1280]{1,0:T(8,128)(2,1)} %v_ref.1), custom_call_target="tpu_custom_call" | custom-call | tf_op jit(solution)/shard_map/pallas_call | solution.py:265
  19.6 0.7 %copy.5 = bf16[48,1280]{1,0:T(8,128)(2,1)} copy(bf16[48,1280]{1,0:T(8,128)(2,1)S(1)} %shard_map.37) | data formatting | bytes 245760

commit v14 on v13

--- a/solution.py
+++ b/solution.py
@@ -232,12 +232,12 @@
     for g in range(whole):
         for start, (weights, scale) in zip((0, half), softened[g]):
             ow[g, pl.ds(start, weights.shape[0]), :] = mix(weights, scale, got[g, 2])
-    for g in range(whole):
-        for b in range(members):
-            put(
-                ow.at[g, pl.ds(b * rows, rows), :], out_ref.at[:, head_cols(me * whole + g)],
-                b == me, where(b), out_send_sem, out_sem,
-            )
+            for b in range(start // rows, (start + weights.shape[0]) // rows):
+                put(
+                    ow.at[g, pl.ds(b * rows, rows), :],
+                    out_ref.at[:, head_cols(me * whole + g)],
+                    b == me, where(b), out_send_sem, out_sem,
+                )
 
     for copy in sent:
         copy.wait_send()

time: 20.4 us -> 20.4 us (level)
  no operation moved by 1% of the time
where the time goes in v14:
time: 20.4 us; the launch traced here: 20.3 us
  Pallas kernels  19.6 us (96%)
  local copies, waits for them, and re-layouts  0.65 us (3%)
    pallas_call x1, Pallas kernels, exchanged(): pl.pallas_call(partial(exchange_kernel, blks, teams, cores, whole, rest),...  19.6 us
    unnamed x1, local copies, waits for them, and re-layouts  0.65 us

profile of v14, /device:TPU:0, one launch (start us, length us, event | category | flops | bytes accessed | tf_op | source)
XLA Modules:
  0.0 20.3 jit_solution(6988104831856327482)
XLA Ops:
  0.0 19.6 %shard_map.37 = bf16[48,1280]{1,0:T(8,128)(2,1)S(1)} custom-call(bf16[48,1280]{1,0:T(8,128)(2,1)} %q_ref.1, bf16[48,1280]{1,0:T(8,128)(2,1)} %k_ref.1, bf16[48,1280]{1,0:T(8,128)(2,1)} %v_ref.1), custom_call_target="tpu_custom_call" | custom-call | tf_op jit(solution)/shard_map/pallas_call | solution.py:265
  19.6 0.7 %copy.5 = bf16[48,1280]{1,0:T(8,128)(2,1)} copy(bf16[48,1280]{1,0:T(8,128)(2,1)S(1)} %shard_map.37) | data formatting | bytes 245760
